TPU v7x, 512 devices: a whole 4x8x8 slice. The times are simulated.
512 devices in a mesh: req: 32 (over z, y_lo), tp: 16 (over x, y_hi, core).
Axes of the slice: x: 4, y: 8 (y_hi: 2, y_lo: 4; y = y_hi * 4 + y_lo), z: 8, core: 2. Of those that a mesh axis runs over, the one named last changes fastest.
Arguments:
- scan_state: float32 [128, 128, 64, 128], P('req', 'tp'), may hold values from -6 to 6
- decay_rate: float32 [128], P('tp'), may hold values from 0.05 to 3
- step_bias: float32 [128], P('tp'), may hold values from -2 to 1
- skip_gain: float32 [128], P('tp'), may hold values from 0.5 to 2
- norm_gain: float32 [128, 64], P('tp'), may hold values from 0.1 to 1.9
- page_pool: bfloat16 [8192, 16, 2048], P(('req', 'tp')), may hold values from -26 to 26
- old_table: int32 [128, 4, 16], P('req', None, 'tp'), may hold values from 0 to 15, as said below
- new_table: int32 [128, 4, 16], P('req', None, 'tp'), may hold values from 0 to 15, as said below
- request_source: int32 [128], replicated, may hold values from 0 to 127, as said below
- head_source: int32 [128], replicated, may hold values from 0 to 127, as said below
- context_lengths: int32 [128], replicated, may hold values from 1 to 1022
- mixer_input: bfloat16 [2, 128, 8192], P(None, 'req', 'tp'), may hold values from -6 to 6
- mixer_gate: bfloat16 [2, 128, 8192], P(None, 'req', 'tp'), may hold values from -6 to 6
- step_raw: float32 [2, 128, 128], P(None, 'req', 'tp'), may hold values from -4 to 4
- state_maps: bfloat16 [2, 128, 2, 1024], P(None, 'req'), may hold values from -4 to 4
- queries: bfloat16 [2, 128, 8192], P(None, 'req'), may hold values from -26 to 26
- new_entries: bfloat16 [2, 128, 2048], P(None, 'req'), may hold values from -26 to 26
Outputs:
- mixer_out: bfloat16 [2, 128, 8192], P(None, 'req', 'tp')
- attention: bfloat16 [2, 128, 8192], P(None, 'req', 'tp')
- final_state: float32 [128, 128, 64, 128], P('req', 'tp')
- final_pool: bfloat16 [8192, 16, 2048], P(('req', 'tp'))
Inputs may be any that keep to these rules, and one draw needn't show every extreme that they name: `request_source`: A permutation: new row p belongs to owner p // 4; its old row belongs to that owner or to one next to it along req. Across each boundary between neighbouring owners the same number of requests moves each way, at most 2, and in every draw some boundary carries exactly 2 each way. `head_source`: A permutation: new slot j belongs to tp index j // 8; its old head belongs to that index or to one next to it. Across each boundary the same number of heads moves each way, at most 4, and in every draw some boundary carries exactly 4 each way. `old_table`: for each owner along req and each tp index t, the entries [p, :, t] of the owner's 4 rows form a permutation of its 16 slots. `new_table`: for each owner along req and each tp index t, the entries [p, :, t] of the owner's 4 rows form a permutation of its 16 slots.
All inputs are finite; a program needn't handle non-finite values.
Results may differ from a plain program's by a relative error of at most 0.0055.
Values may be sent and summed in bfloat16 or wider, within the bound.
A program may use at most 64 MiB of HBM per device.

v0:
```python
import math

import jax
import jax.numpy as jnp
from jax import lax
from jax.sharding import PartitionSpec as P

H = 128
P_SIZE = 64
N = 128
G = 8
QH = 64
KVH = 8
HD = 128
STEPS = 2


EPSILON = 1e-05
HIGH = lax.Precision.HIGHEST


def padded(x, sides, width):
    for axis, dim in sides:
        count, length = (lax.axis_size(axis), x.shape[dim])
        up = [(i, (i + 1) % count) for i in range(count - 1)]
        down = [(j, i) for i, j in up]
        last = lax.slice_in_dim(x, length - width, length, axis=dim)
        leading = lax.slice_in_dim(x, 0, width, axis=dim)
        before = lax.ppermute(last, axis, up)
        after = lax.ppermute(leading, axis, down)
        x = jnp.concatenate([before, x, after], axis=dim)
    return x


def whole_pick(source, block, width):
    wanted = lax.dynamic_slice_in_dim(source, block * width, width)
    return wanted - (block - 1) * width


def per_device(
    scan_state,
    decay_rate,
    step_bias,
    skip_gain,
    norm_gain,
    page_pool,
    old_table,
    new_table,
    request_source,
    head_source,
    context_lengths,
    mixer_input,
    mixer_gate,
    step_raw,
    state_maps,
    queries,
    new_entries,
):
    rows_dev = scan_state.shape[0]
    heads_dev = scan_state.shape[1]
    page_len = page_pool.shape[1]
    kv_width = page_pool.shape[2]
    pages_req = old_table.shape[1]
    tensor_count = lax.axis_size("tp")
    head_block = lax.axis_index("tp")
    req_block = lax.axis_index("req")
    params = jnp.concatenate(
        [norm_gain, step_bias[:, None], decay_rate[:, None], skip_gain[:, None]], axis=1
    )[None]
    pages_old = jnp.take(page_pool, old_table[:, :, 0].reshape(-1), axis=0).reshape(
        rows_dev, pages_req, page_len, kv_width
    )
    state_wide, param_wide = (
        padded(scan_state, (("tp", 1),), heads_dev),
        padded(params, (("tp", 1),), heads_dev),
    )
    head_pick = whole_pick(head_source, head_block, heads_dev)
    state_heads = jnp.take(state_wide, head_pick, axis=1)
    param_heads = jnp.take(param_wide, head_pick, axis=1)[0]
    state_rows = padded(state_heads, (("req", 0),), rows_dev)
    page_rows = padded(pages_old, (("req", 0),), rows_dev)
    row_pick = whole_pick(request_source, req_block, rows_dev)
    state_now = jnp.take(state_rows, row_pick, axis=0)
    pages_now = jnp.take(page_rows, row_pick, axis=0)
    head_gain = param_heads[:, :P_SIZE]
    head_bias = param_heads[:, P_SIZE]
    head_rate = param_heads[:, P_SIZE + 1]
    head_skip = param_heads[:, P_SIZE + 2]
    group_of = lax.dynamic_slice_in_dim(head_source, head_block * heads_dev, heads_dev) // (H // G)
    member = (group_of[:, None] == jnp.arange(G, dtype=jnp.int32)[None, :]).astype(jnp.float32)
    lengths_now = jnp.take(
        context_lengths, lax.dynamic_slice_in_dim(request_source, req_block * rows_dev, rows_dev)
    )
    page_index = jnp.arange(pages_req, dtype=jnp.int32)
    offsets = jnp.arange(page_len, dtype=jnp.int32)
    key_position = (
        (page_index[:, None] * tensor_count + head_block) * page_len + offsets[None, :]
    ).reshape(-1)
    mixer_steps = []
    attention_steps = []
    for decode_step in range(STEPS):
        inputs_now = (
            mixer_input[decode_step].astype(jnp.float32).reshape(rows_dev, heads_dev, P_SIZE)
        )
        gates_now = mixer_gate[decode_step].astype(jnp.float32).reshape(rows_dev, heads_dev, P_SIZE)
        step_size = jax.nn.softplus(step_raw[decode_step] + head_bias[None, :])
        decay = jnp.exp(-head_rate[None, :] * step_size)
        maps_now = state_maps[decode_step].astype(jnp.float32).reshape(rows_dev, 2, G, N)
        head_maps = jnp.einsum("hg,rsgn->rshn", member, maps_now, precision=HIGH)
        state_now = (
            decay[:, :, None, None] * state_now
            + (step_size[:, :, None] * inputs_now)[..., None] * head_maps[:, 0][:, :, None, :]
        )
        mixed = (
            jnp.einsum("rhpn,rhn->rhp", state_now, head_maps[:, 1], precision=HIGH)
            + head_skip[None, :, None] * inputs_now
        )
        gated = mixed * jax.nn.silu(gates_now)
        partial_squares = jnp.dot(jnp.sum(gated * gated, axis=2), member, precision=HIGH)
        group_squares = lax.psum(partial_squares, "tp")
        scale = lax.rsqrt(
            jnp.dot(group_squares / (H // G * P_SIZE), member.T, precision=HIGH) + EPSILON
        )
        mixer_steps.append(
            (gated * scale[..., None] * head_gain[None])
            .astype(jnp.bfloat16)
            .reshape(rows_dev, heads_dev * P_SIZE)
        )
        position = lengths_now + decode_step
        logical = position // page_len
        owned = logical % tensor_count == head_block
        write_mask = (
            owned[:, None, None]
            & (page_index[None, :, None] == (logical // tensor_count)[:, None, None])
            & (offsets[None, None, :] == (position % page_len)[:, None, None])
        )
        pages_now = jnp.where(
            write_mask[..., None], new_entries[decode_step][:, None, None, :], pages_now
        )
        entries = pages_now.reshape(rows_dev, pages_req * page_len, 2, KVH, HD)
        queries_now = queries[decode_step].reshape(rows_dev, KVH, QH // KVH, HD)
        scores = jnp.einsum(
            "rgqd,rsgd->rgqs", queries_now, entries[:, :, 0], preferred_element_type=jnp.float32
        ) * (1.0 / math.sqrt(HD))
        visible = key_position[None, :] <= position[:, None]
        masked = jnp.where(visible[:, None, None, :], scores, -jnp.inf)
        score_peak = lax.pmax(jnp.max(masked, axis=3), "tp")
        weights = jnp.exp(masked - score_peak[..., None]).astype(jnp.bfloat16)
        totals = jnp.sum(weights.astype(jnp.float32), axis=3).reshape(rows_dev, QH)
        numerator = jnp.einsum(
            "rgqs,rsgd->rgqd", weights, entries[:, :, 1], preferred_element_type=jnp.float32
        ).reshape(rows_dev, QH * HD)
        numerator_all, totals_all = lax.psum((numerator, totals), "tp")
        heads_share = QH // tensor_count
        numerator_mine = lax.dynamic_slice_in_dim(
            numerator_all, head_block * heads_share * HD, heads_share * HD, 1
        )
        totals_mine = lax.dynamic_slice_in_dim(totals_all, head_block * heads_share, heads_share, 1)
        heads_here = totals_mine.shape[1]
        attention_steps.append(
            (numerator_mine.reshape(rows_dev, heads_here, HD) / totals_mine[..., None])
            .astype(jnp.bfloat16)
            .reshape(rows_dev, heads_here * HD)
        )
    slots_now = new_table[:, :, 0].reshape(-1)
    final_pool = (
        jnp.zeros(page_pool.shape, jnp.bfloat16)
        .at[slots_now]
        .set(pages_now.reshape(-1, page_len, kv_width))
    )
    return (jnp.stack(mixer_steps), jnp.stack(attention_steps), state_now, final_pool)


def solution(mesh):
    return jax.shard_map(
        per_device,
        mesh=mesh,
        in_specs=(
            P("req", "tp", None, None),
            P("tp"),
            P("tp"),
            P("tp"),
            P("tp", None),
            P(("req", "tp"), None, None),
            P("req", None, "tp"),
            P("req", None, "tp"),
            P(),
            P(),
            P(),
            P(None, "req", "tp"),
            P(None, "req", "tp"),
            P(None, "req", "tp"),
            P(None, "req", None, None),
            P(None, "req", None),
            P(None, "req", None),
        ),
        out_specs=(
            P(None, "req", "tp"),
            P(None, "req", "tp"),
            P("req", "tp", None, None),
            P(("req", "tp"), None, None),
        ),
        check_vma=False,
    )
```

profile of v0, /device:TPU:1, one launch (start us, length us, event | category | flops | bytes accessed | tf_op | source)
XLA Modules:
  0.0 428.2 jit_solution(3927837208716498573)
XLA Ops:
  7.3 8.9 %collective-permute-start.3 = (f32[4,8,64,128]{3,2,1,0:T(8,128)}, f32[4,8,64,128]{3,2,1,0:T(8,128)}, u32[]{:S(2)}, u32[]{:S(2)}) collective-permute-start(f32[4,8,64,128]{3,2,1,0:T(8,128)} %param.17), channel_id=1, source_target_pairs={{1,0},{2,1},{3,2},{4,3},{5,4},{6,5},{7,6},{8,7},{9,8},{10,9},{11,1... | collective-permute-start | bytes 3145736 | tf_op jit(solution)/shard_map/ppermute | solution.py:30
  16.2 2.0 collective-permute-start.2
  21.8 3.3 collective-permute-start.1
  25.1 6.1 %collective-permute-start = (f32[1,8,67]{2,1,0:T(8,128)}, f32[1,8,67]{2,1,0:T(8,128)}, u32[]{:S(2)}, u32[]{:S(2)}) collective-permute-start(f32[1,8,67]{2,1,0:T(8,128)} %maximum_bitcast_fusion.1), channel_id=1, source_target_pairs={{0,1},{1,2},{2,3},{3,4},{4,5},{5,6},{6,7},{7,8},{8,9},{9,10},{10,1... | collective-permute-start | bytes 6440 | tf_op jit(solution)/shard_map/ppermute | solution.py:29
  45.7 18.7 %collective-permute-start.6 = (bf16[4,4,16,2048]{3,2,1,0:T(8,128)(2,1)S(1)}, bf16[4,4,16,2048]{3,2,1,0:T(8,128)(2,1)}, u32[]{:S(2)}, u32[]{:S(2)}) collective-permute-start(bf16[4,4,16,2048]{3,2,1,0:T(8,128)(2,1)S(1)} %broadcast_select_fusion.1), channel_id=1, source_target_pairs={{0,16},{16,32},{32,48},{48,64},{64,80},{80,96},{96,112},{112,128},... | collective-permute-start | bytes 3145736 | tf_op jit(solution)/shard_map/ppermute | solution.py:29
  68.5 3.9 pad_maximum_fusion
  72.4 2.6 gather_fusion.1
  75.0 1.8 select_bitcast_fusion
  78.1 6.0 %collective-permute-start.4 = (f32[4,8,64,128]{3,2,0,1:T(8,128)}, f32[4,8,64,128]{3,2,0,1:T(8,128)}, u32[]{:S(2)}, u32[]{:S(2)}) collective-permute-start(f32[4,8,64,128]{3,2,0,1:T(8,128)} %select_bitcast_fusion), channel_id=1, source_target_pairs={{0,16},{16,32},{32,48},{48,64},{64,80},{80,96},{96,112},{112,128},... | collective-permute-start | bytes 3145736 | tf_op jit(solution)/shard_map/ppermute | solution.py:29
  84.1 2.3 collective-permute-done.6
  86.5 3.0 pad_maximum_fusion.2
  89.5 2.5 gather_fusion.5
  96.2 100.7 %all-reduce.2 = (f32[4,8,8]{2,1,0:T(8,128)}, f32[4,8,8]{2,1,0:T(8,128)}) all-reduce(f32[4,8,8]{2,1,0:T(8,128)} %get-tuple-element.63, f32[4,8,8]{2,1,0:T(8,128)} %get-tuple-element.65), channel_id=1, replica_groups=mesh['req'=32,'tp'=16] {'tp'}, use_global_device_ids=true, to_apply=%region_10.11 | all-reduce | flops 512 | bytes 4096 | tf_op jit(solution)/shard_map/pmax | solution.py:147
  196.8 1.5 convert_reduce_fusion
  198.4 1.5 convert_reduce_fusion.1
  199.9 1.4 reshape.706
  201.3 1.4 reshape.704
  208.9 2.6 pad_maximum_fusion.1
  211.5 2.0 copy.35
  213.7 2.7 gather_fusion.2
  216.4 1.9 fusion.9
  219.2 1.7 fusion.53
  221.5 51.4 %all-reduce = (f32[4,8]{1,0:T(4,128)S(1)}, f32[4,8]{1,0:T(4,128)S(1)}, f32[4,64]{1,0:T(4,128)S(1)}, f32[4,64]{1,0:T(4,128)S(1)}) all-reduce(f32[4,8]{1,0:T(4,128)S(1)} %fusion.21, f32[4,8]{1,0:T(4,128)S(1)} %fusion.22, f32[4,64]{1,0:T(4,128)S(1)} %copy-done.25, f32[4,64]{1,0:T(4,128)S(1)} %copy-done.26), channel_id=1, replica_groups=mesh['req'=32,'tp'=16] {'tp'}, use_global_device_ids=true, to_apply=%region_3.4 | all-reduce | flops 576 | bytes 4608 | tf_op jit(solution)/shard_map/psum | solution.py:120
  274.5 144.8 %all-reduce.5.cloned.1.call-done = (f32[4,8192]{1,0:T(4,128)}, f32[4,8192]{1,0:T(4,128)}) async-done(((f32[4,8192]{1,0:T(4,128)}, f32[4,8192]{1,0:T(4,128)}), (f32[4,8192]{1,0:T(4,128)}, f32[4,8192]{1,0:T(4,128)})) %all-reduce.5.cloned.1.call-update) | async-done | bytes 262160 | tf_op jit(solution)/shard_map/psum | solution.py:153
  (191 shorter events, 38.5 us)
Async XLA Ops:
  7.2 28.8 %copy-start.23 = (bf16[2,4,512]{2,1,0:T(4,128)(2,1)S(1)}, bf16[2,4,512]{2,1,0:T(4,128)(2,1)}, u32[]{:S(2)}) copy-start(bf16[2,4,512]{2,1,0:T(4,128)(2,1)} %param.29) | copy-start | bytes 24580
  7.2 28.9 %copy-start.19 = (bf16[2,4,2,1024]{3,2,1,0:T(2,128)(2,1)S(1)}, bf16[2,4,2,1024]{3,2,1,0:T(2,128)(2,1)}, u32[]{:S(2)}) copy-start(bf16[2,4,2,1024]{3,2,1,0:T(2,128)(2,1)} %param.31) | copy-start | bytes 98308
  7.2 28.9 %copy-start.35 = (s32[128]{0:T(128)S(1)}, s32[128]{0:T(128)}, u32[]{:S(2)}) copy-start(s32[128]{0:T(128)} %param.26) | copy-start | bytes 1540
  7.2 29.6 %copy-start.24 = (bf16[2,4,512]{2,1,0:T(4,128)(2,1)S(1)}, bf16[2,4,512]{2,1,0:T(4,128)(2,1)}, u32[]{:S(2)}) copy-start(bf16[2,4,512]{2,1,0:T(4,128)(2,1)} %param.28) | copy-start | bytes 24580
  7.2 29.7 %copy-start.7 = (bf16[2,4,8192]{2,1,0:T(4,128)(2,1)S(1)}, bf16[2,4,8192]{2,1,0:T(4,128)(2,1)}, u32[]{:S(2)}) copy-start(bf16[2,4,8192]{2,1,0:T(4,128)(2,1)} %param.32) | copy-start | bytes 393220
  7.2 30.3 %copy-start.33 = (s32[128]{0:T(128)S(1)}, s32[128]{0:T(128)}, u32[]{:S(2)}) copy-start(s32[128]{0:T(128)} %param.25) | copy-start | bytes 1540
  7.2 30.4 %copy-start.1 = (s32[128]{0:T(128)S(1)}, s32[128]{0:T(128)}, u32[]{:S(2)}) copy-start(s32[128]{0:T(128)} %param.27) | copy-start | bytes 1540
  7.3 31.8 %copy-start.18 = (bf16[2,4,2048]{2,1,0:T(4,128)(2,1)S(1)}, bf16[2,4,2048]{2,1,0:T(4,128)(2,1)}, u32[]{:S(2)}) copy-start(bf16[2,4,2048]{2,1,0:T(4,128)(2,1)} %param.33) | copy-start | bytes 98308
  7.3 32.0 %copy-start.34 = (s32[4,4,1]{1,2,0:T(1,128)S(1)}, s32[4,4,1]{1,2,0:T(1,128)}, u32[]{:S(2)}) copy-start(s32[4,4,1]{1,2,0:T(1,128)} %param.24) | copy-start | bytes 196
  7.3 412.0 %all-reduce.5.cloned.1.call-start = ((), (), s32[]{:S(2)}) async-start(), calls=%async_computation | async-start | bytes 524288 | tf_op jit(solution)/shard_map/psum | solution.py:153
  7.3 61.1 %collective-permute-start.3 = (f32[4,8,64,128]{3,2,1,0:T(8,128)}, f32[4,8,64,128]{3,2,1,0:T(8,128)}, u32[]{:S(2)}, u32[]{:S(2)}) collective-permute-start(f32[4,8,64,128]{3,2,1,0:T(8,128)} %param.17), channel_id=1, source_target_pairs={{1,0},{2,1},{3,2},{4,3},{5,4},{6,5},{7,6},{8,7},{9,8},{10,9},{11,1... | collective-permute-start | bytes 3145736 | tf_op jit(solution)/shard_map/ppermute | solution.py:30
  16.2 52.2 %collective-permute-start.2 = (f32[4,8,64,128]{3,2,1,0:T(8,128)}, f32[4,8,64,128]{3,2,1,0:T(8,128)}, u32[]{:S(2)}, u32[]{:S(2)}) collective-permute-start(f32[4,8,64,128]{3,2,1,0:T(8,128)} %param.17), channel_id=1, source_target_pairs={{0,1},{1,2},{2,3},{3,4},{4,5},{5,6},{6,7},{7,8},{8,9},{9,10},{10,1... | collective-permute-start | bytes 3145736 | tf_op jit(solution)/shard_map/ppermute | solution.py:29
  21.8 23.9 %collective-permute-start.1 = (f32[1,8,67]{2,1,0:T(8,128)}, f32[1,8,67]{2,1,0:T(8,128)}, u32[]{:S(2)}, u32[]{:S(2)}) collective-permute-start(f32[1,8,67]{2,1,0:T(8,128)} %maximum_bitcast_fusion.1), channel_id=1, source_target_pairs={{1,0},{2,1},{3,2},{4,3},{5,4},{6,5},{7,6},{8,7},{9,8},{10,9},{11,1... | collective-permute-start | bytes 6440 | tf_op jit(solution)/shard_map/ppermute | solution.py:30
  25.1 39.3 %collective-permute-start = (f32[1,8,67]{2,1,0:T(8,128)}, f32[1,8,67]{2,1,0:T(8,128)}, u32[]{:S(2)}, u32[]{:S(2)}) collective-permute-start(f32[1,8,67]{2,1,0:T(8,128)} %maximum_bitcast_fusion.1), channel_id=1, source_target_pairs={{0,1},{1,2},{2,3},{3,4},{4,5},{5,6},{6,7},{7,8},{8,9},{9,10},{10,1... | collective-permute-start | bytes 6440 | tf_op jit(solution)/shard_map/ppermute | solution.py:29
  34.7 49.4 %collective-permute-start.7 = (bf16[4,4,16,2048]{3,2,1,0:T(8,128)(2,1)S(1)}, bf16[4,4,16,2048]{3,2,1,0:T(8,128)(2,1)}, u32[]{:S(2)}, u32[]{:S(2)}) collective-permute-start(bf16[4,4,16,2048]{3,2,1,0:T(8,128)(2,1)S(1)} %broadcast_select_fusion.1), channel_id=1, source_target_pairs={{16,0},{32,16},{48,32},{64,48},{80,64},{96,80},{112,96},{128,112},... | collective-permute-start | bytes 3145736 | tf_op jit(solution)/shard_map/ppermute | solution.py:30
  36.8 31.6 %copy-start.31 = (pred[8]{0:T(512)(128)(4,1)}, pred[8]{0:T(512)(128)(4,1)S(1)}, u32[]{:S(2)}) copy-start(pred[8]{0:T(512)(128)(4,1)S(1)} %get-tuple-element.34) | copy-start | bytes 28
  36.8 31.6 %copy-start.28 = (s32[1024]{0:T(1024)}, s32[1024]{0:T(1024)S(1)}, u32[]{:S(2)}) copy-start(s32[1024]{0:T(1024)S(1)} %pad_clamp_fusion.3) | copy-start | bytes 12292
  43.2 49.0 %copy-start.29 = (pred[4]{0:T(512)(128)(4,1)}, pred[4]{0:T(512)(128)(4,1)S(1)}, u32[]{:S(2)}) copy-start(pred[4]{0:T(512)(128)(4,1)S(1)} %get-tuple-element.28) | copy-start | bytes 16
  43.2 46.3 %copy-start.27 = (s32[1024]{0:T(1024)}, s32[1024]{0:T(1024)S(1)}, u32[]{:S(2)}) copy-start(s32[1024]{0:T(1024)S(1)} %pad_clamp_fusion.2) | copy-start | bytes 12292
  45.7 40.7 %collective-permute-start.6 = (bf16[4,4,16,2048]{3,2,1,0:T(8,128)(2,1)S(1)}, bf16[4,4,16,2048]{3,2,1,0:T(8,128)(2,1)}, u32[]{:S(2)}, u32[]{:S(2)}) collective-permute-start(bf16[4,4,16,2048]{3,2,1,0:T(8,128)(2,1)S(1)} %broadcast_select_fusion.1), channel_id=1, source_target_pairs={{0,16},{16,32},{32,48},{48,64},{64,80},{80,96},{96,112},{112,128},... | collective-permute-start | bytes 3145736 | tf_op jit(solution)/shard_map/ppermute | solution.py:29
  76.8 132.0 %collective-permute-start.5 = (f32[4,8,64,128]{3,2,0,1:T(8,128)}, f32[4,8,64,128]{3,2,0,1:T(8,128)}, u32[]{:S(2)}, u32[]{:S(2)}) collective-permute-start(f32[4,8,64,128]{3,2,0,1:T(8,128)} %select_bitcast_fusion), channel_id=1, source_target_pairs={{16,0},{32,16},{48,32},{64,48},{80,64},{96,80},{112,96},{128,112},... | collective-permute-start | bytes 3145736 | tf_op jit(solution)/shard_map/ppermute | solution.py:30
  78.1 130.7 %collective-permute-start.4 = (f32[4,8,64,128]{3,2,0,1:T(8,128)}, f32[4,8,64,128]{3,2,0,1:T(8,128)}, u32[]{:S(2)}, u32[]{:S(2)}) collective-permute-start(f32[4,8,64,128]{3,2,0,1:T(8,128)} %select_bitcast_fusion), channel_id=1, source_target_pairs={{0,16},{16,32},{32,48},{48,64},{64,80},{80,96},{96,112},{112,128},... | collective-permute-start | bytes 3145736 | tf_op jit(solution)/shard_map/ppermute | solution.py:29
  213.7 59.7 %copy-start.9 = (f32[8,67]{1,0:T(8,128)S(1)}, f32[8,67]{1,0:T(8,128)}, u32[]{:S(2)}) copy-start(f32[8,67]{1,0:T(8,128)} %copy-done.8) | copy-start | bytes 6436
  219.2 202.1 %copy-start.2 = (f32[4,8,64,128]{3,2,1,0:T(8,128)}, f32[4,8,64,128]{3,2,1,0:T(8,128)S(1)}, u32[]{:S(2)}) copy-start(f32[4,8,64,128]{3,2,1,0:T(8,128)S(1)} %multiply_add_fusion) | copy-start | bytes 3145732
  (25 other events, 162.6 us)
Sparse Core Ops, SparseCore 0:
  206.7 212.5 all-reduce.4
where the time goes:
time: 430 us; the launch traced here: 428 us
  blocking collectives  152 us (35%)
  waiting for transfers between devices  147 us (34%)
  starting transfers between devices  47.6 us (11%)
  other arithmetic  31.2 us (7%)
  local copies, waits for them, and re-layouts  26.1 us (6%)
  between operations  14.8 us (3%)
  matrix products  9.23 us (2%)
    psum x1, waiting for transfers between devices, per_device(): numerator_all, totals_all = lax.psum((numerator, totals), 'tp')  145 us
    pmax x1, blocking collectives, per_device(): score_peak = lax.pmax(jnp.max(masked, axis=3), 'tp')  101 us
    psum x1, blocking collectives, per_device(): group_squares = lax.psum(partial_squares, 'tp')  51.4 us
    ppermute x4, starting transfers between devices, padded(): before = lax.ppermute(last, axis, up)  32.8 us
    ppermute x4, starting transfers between devices, padded(): after = lax.ppermute(leading, axis, down)  14.8 us
    concatenate x4, other arithmetic, padded(): x = jnp.concatenate([before, x, after], axis=dim)  10.3 us
  transfers between devices with their start and end apart: 9, of which 2 were waited for; matrix products, arithmetic and copies ran while one was open for 15% of the time, Pallas kernels for 0%

commit v1 on v0

v1 whole, which is shorter than its diff:
```python
import math

import jax
import jax.numpy as jnp
from jax import lax
from jax.experimental import pallas as pl
from jax.experimental.pallas import tpu as pltpu
from jax.sharding import PartitionSpec as P

MESH = pl.DeviceIdType.MESH
HIGH = lax.Precision.HIGHEST
F32 = jnp.float32
BF16 = jnp.bfloat16
I32 = jnp.int32

P_SIZE = 64
N = 128
G = 8
QH = 64
KVH = 8
HD = 128
PAGE = 16
STEPS = 2
ROWS = 4
PGS = 4
MV = 2
HPD = 8
HMV = 4
HEADS_PER_GROUP = 16
GROUP_CHANNELS = 1024
KVW = 2048
SLOTS = ROWS * PGS
SI = STEPS * ROWS
CH = HPD * P_SIZE
NEG = -1e30
EPSILON = 1e-05

T_AR, T_AL, T_HEAD, T_BR, T_BL, T_ROW = 0, 4, 8, 16, 18, 20
T_OWNPG, T_RECVPG, T_ISOWN, T_INV, T_GROUP, T_LEN, T_PAR = 24, 40, 56, 60, 76, 84, 88


def dot_nt(a, b, precision=None):
    return lax.dot_general(
        a, b, (((1,), (1,)), ((), ())), precision=precision, preferred_element_type=F32
    )


def choose(source, base, count, block, most):
    picks = [jnp.int32(0)] * most
    seen = jnp.int32(0)
    for i in range(count):
        v = source[base + i]
        hit = v // count == block
        for k in range(most):
            picks[k] = jnp.where(hit & (seen == k), v - block * count, picks[k])
        seen = seen + hit.astype(I32)
    return picks


def kernel(ntp, nreq, *refs):
    (
        state_hbm, gain_hbm, pool_hbm, x_hbm, gate_hbm, maps_hbm, q_hbm, entry_hbm,
        raw_hbm, rate_h, bias_h, skip_h, old_h, new_h, rsrc_h, hsrc_h, ctx_h,
        mixer_hbm, attn_hbm, state_out, pool_out,
        own, a_send, a_recv, rowbuf, b_send, b_recv, pool_v, c_send, c_recv, newp, fin_pool, fin_state,
        gain_in, x_in, gate_in, maps_in, q_in, entry_in,
        p_own, p_recv, p_gain, p_scal, slot_scal, dt_v, decay_v, raw_t,
        xf, xpad, x_t, qf, ef, maps_f, maps_g, c_rows, outer, member, skip_row, gain_row, stash, ybuf,
        vis, x_send, x_recv, l_send, l_recv, s_send, s_recv, mixer_v, attn_v, raw_in,
        rate_s, bias_s, skip_s, old_s, new_s, rsrc, hsrc, ctx, tab,
        in_sem, scalar_sem, a_ss, a_rs, p_ss, p_rs, b_ss, b_rs, c_ss, c_rs, x_ss, x_rs, l_ss, l_rs, s_ss, s_rs, out_sem,
    ) = refs
    share = QH // ntp
    xrows = share * SI
    t = lax.axis_index("tp")
    r = lax.axis_index("req")
    t_right, t_left = lax.rem(t + 1, ntp), lax.rem(t + ntp - 1, ntp)
    r_right, r_left = lax.rem(r + 1, nreq), lax.rem(r + nreq - 1, nreq)
    dev = {"tr": (r, t_right), "tl": (r, t_left), "rr": (r_right, t), "rl": (r_left, t)}

    scalars = [
        pltpu.make_async_copy(src, dst, scalar_sem.at[k])
        for k, (src, dst) in enumerate(
            (
                (hsrc_h, hsrc), (rsrc_h, rsrc), (old_h, old_s), (ctx_h, ctx), (new_h, new_s),
                (rate_h, rate_s), (bias_h, bias_s), (skip_h, skip_s),
            )
        )
    ]
    loads = [
        pltpu.make_async_copy(state_hbm, own.at[:, pl.ds(0, HPD)], in_sem.at[0]),
        pltpu.make_async_copy(pool_hbm, pool_v, in_sem.at[1]),
        pltpu.make_async_copy(gain_hbm, gain_in, in_sem.at[2]),
        pltpu.make_async_copy(x_hbm, x_in, in_sem.at[3]),
        pltpu.make_async_copy(gate_hbm, gate_in, in_sem.at[4]),
        pltpu.make_async_copy(maps_hbm, maps_in, in_sem.at[5]),
        pltpu.make_async_copy(q_hbm, q_in, in_sem.at[6]),
        pltpu.make_async_copy(entry_hbm, entry_in, in_sem.at[7]),
        pltpu.make_async_copy(raw_hbm, raw_in, in_sem.at[8]),
    ]
    for c in scalars + loads:
        c.start()

    barrier = pltpu.get_barrier_semaphore()
    for name in ("rr", "rl"):
        pl.semaphore_signal(barrier, inc=1, device_id=dev[name], device_id_type=MESH)

    def greet(k, _):
        pl.semaphore_signal(
            barrier, inc=1, device_id=(r, lax.rem(t + k, ntp)), device_id_type=MESH
        )
        return 0

    lax.fori_loop(1, ntp, greet, 0)

    with jax.named_scope("scalars"):
        for c in scalars:
            c.wait()
    for k, v in enumerate(choose(hsrc, t_right * HPD, HPD, t, HMV)):
        tab[T_AR + k] = v
    for k, v in enumerate(choose(hsrc, t_left * HPD, HPD, t, HMV)):
        tab[T_AL + k] = v
    for k, v in enumerate(choose(rsrc, r_right * ROWS, ROWS, r, MV)):
        tab[T_BR + k] = v
    for k, v in enumerate(choose(rsrc, r_left * ROWS, ROWS, r, MV)):
        tab[T_BL + k] = v
    lefts, rights = jnp.int32(0), jnp.int32(0)
    for j in range(HPD):
        v = hsrc[t * HPD + j]
        far = v // HPD - t
        place = jnp.where(far == 0, v - t * HPD, jnp.where(far < 0, HPD + lefts, HPD + HMV + rights))
        tab[T_HEAD + j] = jnp.clip(place, 0, HPD + 2 * HMV - 1)
        tab[T_PAR + j] = jnp.clip(v - t * HPD + HPD, 0, 3 * HPD - 1)
        tab[T_GROUP + j] = v // HEADS_PER_GROUP
        lefts = lefts + (far < 0).astype(I32)
        rights = rights + (far > 0).astype(I32)
    lefts, rights = jnp.int32(0), jnp.int32(0)
    for i in range(ROWS):
        v = rsrc[r * ROWS + i]
        far = v // ROWS - r
        here = jnp.where(far == 0, v - r * ROWS, 0)
        away = jnp.where(far < 0, lefts, MV + rights)
        away = jnp.clip(jnp.where(far == 0, 0, away), 0, 2 * MV - 1)
        tab[T_ROW + i] = jnp.where(far == 0, here, ROWS + away)
        tab[T_ISOWN + i] = (far == 0).astype(I32)
        tab[T_LEN + i] = ctx[v]
        for g in range(PGS):
            tab[T_OWNPG + i * PGS + g] = old_s[here, 0, g]
            tab[T_RECVPG + i * PGS + g] = away * PGS + g
        lefts = lefts + (far < 0).astype(I32)
        rights = rights + (far > 0).astype(I32)

    loads[0].wait()

    def pack_a(n, _):
        d, k, q = n // (HMV * ROWS), (n // ROWS) % HMV, n % ROWS
        a_send[d, k, q] = own[q, tab[T_AR + d * HMV + k]].astype(BF16)
        return 0

    lax.fori_loop(0, 2 * HMV * ROWS, pack_a, 0)

    loads[2].wait()
    sub = lax.broadcasted_iota(I32, (HPD, N), 0)
    lane = lax.broadcasted_iota(I32, (HPD, N), 1)
    p_own[0:HPD, 0:P_SIZE] = gain_in[...]
    wide = p_own[0:HPD, :]
    p_own[0:HPD, :] = jnp.where(lane < P_SIZE, wide, pltpu.roll(wide, P_SIZE, 1))
    scal = jnp.zeros((HPD, N), F32)
    for h in range(HPD):
        for place, ref in enumerate((bias_s, rate_s, skip_s)):
            scal = jnp.where((sub == h) & (lane == place), ref[h], scal)
    p_own[HPD : 2 * HPD, :] = scal

    with jax.named_scope("entry_barrier"):
        pl.semaphore_wait(barrier, ntp + 1)

    def send(src, dst, ss, rs, to):
        return pltpu.make_async_remote_copy(
            src_ref=src, dst_ref=dst, send_sem=ss, recv_sem=rs, device_id=to, device_id_type=MESH
        )

    a_cp = [
        send(a_send.at[d], a_recv.at[d], a_ss.at[d], a_rs.at[d], dev[("tr", "tl")[d]])
        for d in range(2)
    ]
    p_cp = [
        send(p_own, p_recv.at[d], p_ss.at[d], p_rs.at[d], dev[("tr", "tl")[d]]) for d in range(2)
    ]
    for c in p_cp + a_cp:
        c.start()

    loads[1].wait()

    def pack_c(n, _):
        d, k, g = n // (MV * PGS), (n // PGS) % MV, n % PGS
        c_send[n] = pool_v[old_s[tab[T_BR + d * MV + k], 0, g]]
        return 0

    c_cp = []
    for d in range(2):
        lax.fori_loop(d * MV * PGS, (d + 1) * MV * PGS, pack_c, 0)
        part = pl.ds(d * MV * PGS, MV * PGS)
        c = send(c_send.at[part], c_recv.at[part], c_ss.at[d], c_rs.at[d], dev[("rr", "rl")[d]])
        c.start()
        c_cp.append(c)

    for i in range(SLOTS):
        found = jnp.int32(0)
        for e in range(SLOTS):
            found = jnp.where(new_s[e // PGS, 0, e % PGS] == i, e, found)
        tab[T_INV + i] = found
    for c in loads[3:]:
        c.wait()
    xpad[...] = jnp.zeros_like(xpad)
    for s in range(STEPS):
        part = slice(s * ROWS, (s + 1) * ROWS)
        xf[0, part, :] = x_in[s].astype(F32)
        xf[1, part, :] = gate_in[s].astype(F32)
        qf[part, :] = q_in[s].astype(F32)
        ef[part, :] = entry_in[s].astype(F32)
        for i in range(ROWS):
            row = 2 * (s * ROWS + i)
            maps_f[row : row + 2, :] = maps_in[s, i].astype(F32)
    for g in range(G):
        maps_g[g] = maps_f[:, g * N : (g + 1) * N]
    for s in range(STEPS):
        xpad[s * ROWS : (s + 1) * ROWS, 0:HPD] = raw_in[s]
    raw_t[...] = xpad[:, 0:N].T[0:HPD, :]
    xpad[0:SI, :] = xf[0]
    for m in range(CH // N):
        x_t[m * N : (m + 1) * N, :] = xpad[:, m * N : (m + 1) * N].T

    rowid = lax.broadcasted_iota(I32, (QH, ROWS * PGS * PAGE), 0)
    colid = lax.broadcasted_iota(I32, (QH, ROWS * PGS * PAGE), 1)
    row_i = rowid % ROWS
    limit = (rowid // ROWS) % STEPS
    for i in range(ROWS):
        limit = limit + jnp.where(row_i == i, tab[T_LEN + i], 0)
    place = ((colid // PAGE) % PGS * ntp + t) * PAGE + colid % PAGE
    seen = (row_i == colid // (PGS * PAGE)) & (place <= limit)
    vis[...] = jnp.where(seen, 1.0, 0.0)

    with jax.named_scope("params_arrive"):
        for c in p_cp:
            c.wait_recv()
    for part, buf in enumerate((p_gain, p_scal)):
        rows = slice(part * HPD, (part + 1) * HPD)
        buf[0:HPD, :] = p_recv[0, rows, :]
        buf[HPD : 2 * HPD, :] = p_own[rows, :]
        buf[2 * HPD : 3 * HPD, :] = p_recv[1, rows, :]
    for j in range(HPD):
        slot_scal[j : j + 1, :] = p_scal[pl.ds(tab[T_PAR + j], 1), :]
    bias, rate, skip = (slot_scal[:, k : k + 1] for k in range(3))
    v = raw_t[...] + bias
    dt = jnp.maximum(v, 0.0) + jnp.log1p(jnp.exp(-jnp.abs(v)))
    dt_v[...] = dt
    decay_v[...] = jnp.exp(-rate * dt)
    lane1 = lax.broadcasted_iota(I32, (1, N), 1)
    for m in range(CH // N):
        lanes = slice(m * N, (m + 1) * N)
        first = p_gain[pl.ds(tab[T_PAR + 2 * m], 1), :]
        second = p_gain[pl.ds(tab[T_PAR + 2 * m + 1], 1), :]
        gain_row[:, lanes] = jnp.where(lane1 < P_SIZE, first, second)
        skip_row[:, lanes] = jnp.where(
            lane1 < P_SIZE,
            jnp.broadcast_to(skip[2 * m : 2 * m + 1], (1, N)),
            jnp.broadcast_to(skip[2 * m + 1 : 2 * m + 2], (1, N)),
        )
    lane64 = lax.broadcasted_iota(I32, (P_SIZE, N), 1)

    def prepare(j, _):
        group = tab[T_GROUP + j]
        member[pl.ds(pl.multiple_of(j * P_SIZE, P_SIZE), P_SIZE), :] = jnp.where(
            lane64 == group, 1.0, 0.0
        )
        both = maps_g[group]
        dts = dt_v[pl.ds(j, 1), :]
        cols = x_t[pl.ds(pl.multiple_of(j * P_SIZE, P_SIZE), P_SIZE), :]
        for k in range(SI):
            outer[k, j] = cols[:, k : k + 1] * (dts[:, k : k + 1] * both[2 * k : 2 * k + 1, :])
            c_rows[k, pl.ds(j, 1), :] = both[2 * k + 1 : 2 * k + 2, :]
        return 0

    lax.fori_loop(0, HPD, prepare, 0)

    with jax.named_scope("heads_arrive"):
        for c in a_cp:
            c.wait_recv()

    def take_a(n, _):
        k, q = n // ROWS, n % ROWS
        own[q, HPD + k] = a_recv[k // HMV, k % HMV, q].astype(F32)
        return 0

    lax.fori_loop(0, 2 * HMV * ROWS, take_a, 0)

    def take_own(n, _):
        q, j = n // HPD, n % HPD
        rowbuf[q, j] = own[q, tab[T_HEAD + j]]
        return 0

    lax.fori_loop(0, ROWS * HPD, take_own, 0)

    def pack_b(n, _):
        d, k, j = n // (MV * HPD), (n // HPD) % MV, n % HPD
        b_send[d, k, j] = rowbuf[tab[T_BR + d * MV + k], j].astype(BF16)
        return 0

    lax.fori_loop(0, 2 * MV * HPD, pack_b, 0)
    b_cp = [
        send(b_send.at[d], b_recv.at[d], b_ss.at[d], b_rs.at[d], dev[("rr", "rl")[d]])
        for d in range(2)
    ]

    with jax.named_scope("pages_arrive"):
        for c in c_cp:
            c.wait_recv()
    for c in b_cp:
        c.start()
    offset = lax.broadcasted_iota(I32, (PAGE, KVW), 0)

    def take_page(n, _):
        i, g = n // PGS, n % PGS
        mine = pool_v[tab[T_OWNPG + n]].astype(F32)
        came = c_recv[tab[T_RECVPG + n]].astype(F32)
        page = jnp.where(tab[T_ISOWN + i] == 1, mine, came)
        for s in range(STEPS):
            position = tab[T_LEN + i] + s
            logical = position // PAGE
            hit = (logical % ntp == t) & (logical // ntp == g)
            at = jnp.where(hit, position % PAGE, -1)
            page = jnp.where(offset == at, ef[pl.ds(s * ROWS + i, 1), :], page)
        newp[n] = page.astype(BF16)
        return 0

    lax.fori_loop(0, SLOTS, take_page, 0)

    eye = lax.broadcasted_iota(I32, (xrows, N), 0) == lax.broadcasted_iota(I32, (xrows, N), 1)
    shown = vis[...] > 0.5
    per = QH // KVH
    for g in range(KVH):
        q = jnp.concatenate(
            [qf[:, (g * per + h) * HD : (g * per + h + 1) * HD] for h in range(per)], axis=0
        ).astype(BF16)
        keys = newp[:, :, g * HD : (g + 1) * HD].reshape(SLOTS * PAGE, HD)
        values = newp[:, :, (KVH + g) * HD : (KVH + g + 1) * HD].reshape(SLOTS * PAGE, HD)
        scores = jnp.where(shown, dot_nt(q, keys) * (1.0 / math.sqrt(HD)), NEG)
        peak = jnp.max(scores, axis=1, keepdims=True)
        weights = jnp.where(shown, jnp.exp(scores - peak), 0.0).astype(BF16)
        total = jnp.sum(weights.astype(F32), axis=1, keepdims=True)
        part = jnp.dot(weights, values, preferred_element_type=F32)
        safe = jnp.maximum(total, 1e-30)
        part = (part / safe).astype(BF16)
        lse = jnp.where(total > 0.0, peak + jnp.log(safe), NEG)
        for e in range(per // share):
            rows = slice(e * xrows, (e + 1) * xrows)
            x_send[g * (per // share) + e] = part[rows]
            l_send[g * (per // share) + e] = jnp.sum(
                jnp.where(eye, lse[rows], 0.0), axis=0, keepdims=True
            )

    def x_copy(k):
        to = lax.rem(t + k, ntp)
        return (
            send(x_send.at[to], x_recv.at[k], x_ss.at[k], x_rs.at[k], (r, to)),
            send(l_send.at[to], l_recv.at[k], l_ss.at[k], l_rs.at[k], (r, to)),
        )

    def x_start(k, _):
        for c in x_copy(k):
            c.start()
        return 0

    lax.fori_loop(1, ntp, x_start, 0)
    x_recv[0] = x_send[t]
    l_recv[0] = l_send[t]

    def place_page(n, _):
        fin_pool[n] = newp[tab[T_INV + n]]
        return 0

    lax.fori_loop(0, SLOTS, place_page, 0)
    outs = [pltpu.make_async_copy(fin_pool, pool_out, out_sem.at[0])]
    outs[0].start()

    def x_wait(k, _):
        for c in x_copy(k):
            c.wait_recv()
        return 0

    with jax.named_scope("partials_arrive"):
        lax.fori_loop(1, ntp, x_wait, 0)
    lses = l_recv[...].reshape(ntp, N)
    w = jnp.exp(lses - jnp.max(lses, axis=0, keepdims=True))
    w = w / jnp.sum(w, axis=0, keepdims=True)
    total = jnp.zeros((xrows, HD), F32)
    for k in range(ntp):
        col = jnp.sum(jnp.where(eye, w[k : k + 1, :], 0.0), axis=1, keepdims=True)
        total = total + col * x_recv[k].astype(F32)
    for s in range(STEPS):
        for h in range(share):
            attn_v[s, :, h * HD : (h + 1) * HD] = total[
                h * SI + s * ROWS : h * SI + (s + 1) * ROWS
            ].astype(BF16)
    outs.append(pltpu.make_async_copy(attn_v, attn_hbm, out_sem.at[1]))
    outs[1].start()

    with jax.named_scope("rows_arrive"):
        for c in b_cp:
            c.wait_recv()

    def take_b(n, _):
        k, j = n // HPD, n % HPD
        rowbuf[ROWS + k, j] = b_recv[k // MV, k % MV, j].astype(F32)
        return 0

    lax.fori_loop(0, 2 * MV * HPD, take_b, 0)
    diagonal = lax.broadcasted_iota(I32, (HPD, CH), 0) == (
        lax.broadcasted_iota(I32, (HPD, CH), 1) // P_SIZE
    )
    for i in range(ROWS):

        def step(j, _):
            now = rowbuf[tab[T_ROW + i], j]
            fade = decay_v[pl.ds(j, 1), :]
            for s in range(STEPS):
                k = s * ROWS + i
                now = fade[:, k : k + 1] * now + outer[k, j]
                stash[s, pl.ds(pl.multiple_of(j * P_SIZE, P_SIZE), P_SIZE), :] = now
            fin_state[i, j] = now
            return 0

        lax.fori_loop(0, HPD, step, 0)
        for s in range(STEPS):
            k = s * ROWS + i
            now = stash[s]
            top = now.astype(BF16)
            low = (now - top.astype(F32)).astype(BF16)
            c8 = c_rows[k].astype(BF16)
            y = dot_nt(c8, top) + dot_nt(c8, low)
            ybuf[k : k + 1, :] = jnp.sum(jnp.where(diagonal, y, 0.0), axis=0, keepdims=True)
    outs.append(pltpu.make_async_copy(fin_state, state_out, out_sem.at[2]))
    outs[2].start()

    gate = xf[1]
    gated = (ybuf[...] + skip_row[...] * xf[0]) * (gate / (1.0 + jnp.exp(-gate)))
    s_send[...] = jnp.dot(gated * gated, member[...], precision=HIGH, preferred_element_type=F32)

    def s_copy(k):
        to = lax.rem(t + k, ntp)
        return send(s_send, s_recv.at[k], s_ss.at[k], s_rs.at[k], (r, to))

    def s_start(k, _):
        s_copy(k).start()
        return 0

    lax.fori_loop(1, ntp, s_start, 0)
    s_recv[0] = s_send[...]

    def s_wait(k, _):
        s_copy(k).wait_recv()
        return 0

    with jax.named_scope("squares_arrive"):
        lax.fori_loop(1, ntp, s_wait, 0)
    squares = jnp.sum(s_recv[...], axis=0)
    scale = lax.rsqrt(squares * (1.0 / GROUP_CHANNELS) + EPSILON)
    mixed = gated * dot_nt(scale, member[...], HIGH) * gain_row[...]
    for s in range(STEPS):
        mixer_v[s] = mixed[s * ROWS : (s + 1) * ROWS].astype(BF16)
    outs.append(pltpu.make_async_copy(mixer_v, mixer_hbm, out_sem.at[3]))
    outs[3].start()

    def last(k, _):
        for c in x_copy(k) + (s_copy(k),):
            c.wait_send()
        return 0

    with jax.named_scope("all_sent"):
        for c in a_cp + p_cp + c_cp + b_cp:
            c.wait_send()
        lax.fori_loop(1, ntp, last, 0)
        for c in outs:
            c.wait()


def per_device(ntp, nreq, *arguments):
    (
        scan_state, decay_rate, step_bias, skip_gain, norm_gain, page_pool, old_table, new_table,
        request_source, head_source, context_lengths, mixer_input, mixer_gate, step_raw, state_maps,
        queries, new_entries,
    ) = arguments
    xrows = QH // ntp * SI
    anywhere = pl.BlockSpec(memory_space=pl.ANY)
    dma = pltpu.SemaphoreType.DMA
    scratch = [
        ((ROWS, HPD + 2 * HMV, P_SIZE, N), F32),
        ((2, HMV, ROWS, P_SIZE, N), BF16),
        ((2, HMV, ROWS, P_SIZE, N), BF16),
        ((ROWS + 2 * MV, HPD, P_SIZE, N), F32),
        ((2, MV, HPD, P_SIZE, N), BF16),
        ((2, MV, HPD, P_SIZE, N), BF16),
        ((SLOTS, PAGE, KVW), BF16),
        ((2 * MV * PGS, PAGE, KVW), BF16),
        ((2 * MV * PGS, PAGE, KVW), BF16),
        ((SLOTS, PAGE, KVW), BF16),
        ((SLOTS, PAGE, KVW), BF16),
        ((ROWS, HPD, P_SIZE, N), F32),
        (norm_gain.shape, F32),
        (mixer_input.shape, BF16),
        (mixer_gate.shape, BF16),
        (state_maps.shape, BF16),
        (queries.shape, BF16),
        (new_entries.shape, BF16),
        ((2 * HPD, N), F32),
        ((2, 2 * HPD, N), F32),
        ((3 * HPD, N), F32),
        ((3 * HPD, N), F32),
        ((HPD, N), F32),
        ((HPD, N), F32),
        ((HPD, N), F32),
        ((HPD, N), F32),
        ((2, SI, CH), F32),
        ((N, CH), F32),
        ((CH, N), F32),
        ((SI, QH * HD), F32),
        ((SI, KVW), F32),
        ((2 * SI, G * N), F32),
        ((G, 2 * SI, N), F32),
        ((SI, HPD, N), F32),
        ((SI, HPD, P_SIZE, N), F32),
        ((CH, N), F32),
        ((1, CH), F32),
        ((1, CH), F32),
        ((STEPS, CH, N), F32),
        ((SI, CH), F32),
        ((QH, SLOTS * PAGE), F32),
        ((ntp, xrows, HD), BF16),
        ((ntp, xrows, HD), BF16),
        ((ntp, 1, N), F32),
        ((ntp, 1, N), F32),
        ((SI, N), F32),
        ((ntp, SI, N), F32),
        ((STEPS, ROWS, CH), BF16),
        ((STEPS, ROWS, CH), BF16),
        (step_raw.shape, F32),
    ]
    return pl.pallas_call(
        lambda *refs: kernel(ntp, nreq, *refs),
        out_shape=(
            jax.ShapeDtypeStruct((STEPS, ROWS, CH), BF16),
            jax.ShapeDtypeStruct((STEPS, ROWS, CH), BF16),
            jax.ShapeDtypeStruct(scan_state.shape, F32),
            jax.ShapeDtypeStruct(page_pool.shape, BF16),
        ),
        in_specs=[pl.BlockSpec(memory_space=pltpu.HBM)] * 17,
        out_specs=(anywhere,) * 4,
        scratch_shapes=[pltpu.VMEM(shape, dtype) for shape, dtype in scratch]
        + [
            *[pltpu.SMEM((HPD,), F32) for _ in range(3)],
            *[pltpu.SMEM((ROWS, 1, PGS), I32) for _ in range(2)],
            *[pltpu.SMEM(ints.shape, I32) for ints in (request_source, head_source, context_lengths)],
            pltpu.SMEM((128,), I32),
            dma((9,)),
            dma((8,)),
            *[dma((2,)) for _ in range(8)],
            *[dma((ntp,)) for _ in range(6)],
            dma((4,)),
        ],
        compiler_params=pltpu.CompilerParams(
            collective_id=0, has_side_effects=True, vmem_limit_bytes=63 * 2**20
        ),
        name="decode",
    )(
        scan_state, norm_gain, page_pool, mixer_input, mixer_gate, state_maps, queries, new_entries,
        step_raw, decay_rate, step_bias, skip_gain, old_table.transpose(0, 2, 1), new_table.transpose(0, 2, 1),
        request_source, head_source, context_lengths,
    )


def solution(mesh):
    ntp, nreq = mesh.shape["tp"], mesh.shape["req"]
    return jax.shard_map(
        lambda *arguments: per_device(ntp, nreq, *arguments),
        mesh=mesh,
        in_specs=(
            P("req", "tp", None, None),
            P("tp"),
            P("tp"),
            P("tp"),
            P("tp", None),
            P(("req", "tp"), None, None),
            P("req", None, "tp"),
            P("req", None, "tp"),
            P(),
            P(),
            P(),
            P(None, "req", "tp"),
            P(None, "req", "tp"),
            P(None, "req", "tp"),
            P(None, "req", None, None),
            P(None, "req", None),
            P(None, "req", None),
        ),
        out_specs=(
            P(None, "req", "tp"),
            P(None, "req", "tp"),
            P("req", "tp", None, None),
            P(("req", "tp"), None, None),
        ),
        check_vma=False,
    )
```

time: 430 us -> 86.1 us (0.20)
  the two profiles are of different devices: /device:TPU:1 before, /device:TPU:217 now
where the time goes in v1:
time: 86.1 us; the launch traced here: 85.9 us
  Pallas kernels  80 us (93%)
  local copies, waits for them, and re-layouts  5.28 us (6%)
    pallas_call x1, Pallas kernels, per_device(): pl.pallas_call(lambda *refs: kernel(ntp, nreq, *refs), out_shape=(jax.Sha...  80 us
    unnamed x8, local copies, waits for them, and re-layouts  5.28 us

profile of v1, /device:TPU:217, one launch (start us, length us, event | category | flops | bytes accessed | tf_op | source)
XLA Modules:
  0.0 85.9 jit_solution(9049034798128916574)
XLA Ops:
  0.6 80.0 %decode.1 = (bf16[2,4,512]{2,1,0:T(4,128)(2,1)}, bf16[2,4,512]{2,1,0:T(4,128)(2,1)}, f32[4,8,64,128]{3,2,1,0:T(8,128)}, bf16[16,16,2048]{2,1,0:T(8,128)(2,1)}) custom-call(f32[4,8,64,128]{3,2,1,0:T(8,128)} %refs_0_.1, f32[8,64]{1,0:T(8,128)} %refs_1_.1, bf16[16,16,2048]{2,1,0:T(8,128)(2,1)} %refs_2_.1, bf16[2,4,512]{2,1,0:T(4,128)(2,1)} %refs_3_.1, ...), custom_call_target="tpu_custom_call" | custom-call | tf_op jit(solution)/shard_map/decode/pallas_call | solution.py:548
  80.6 0.0 copy-start.1
  80.6 1.3 %copy.27 = bf16[2,4,512]{2,1,0:T(4,128)(2,1)} copy(bf16[2,4,512]{2,1,0:T(4,128)(2,1)} %get-tuple-element.8) | data formatting | bytes 16384
  81.9 0.0 copy-done.1
  81.9 0.6 copy.28
  82.5 0.0 copy-start
  82.5 2.4 %copy.29 = f32[4,8,64,128]{3,2,1,0:T(8,128)} copy(f32[4,8,64,128]{3,2,1,0:T(8,128)} %get-tuple-element.10) | data formatting | bytes 2097152
  84.9 0.0 copy-done
  84.9 1.0 %copy.30 = bf16[16,16,2048]{2,1,0:T(8,128)(2,1)} copy(bf16[16,16,2048]{2,1,0:T(8,128)(2,1)S(1)} %copy-done) | data formatting | bytes 2097152
Async XLA Ops:
  80.6 1.3 %copy-start.1 = (bf16[2,4,512]{2,1,0:T(4,128)(2,1)S(1)}, bf16[2,4,512]{2,1,0:T(4,128)(2,1)}, u32[]{:S(2)}) copy-start(bf16[2,4,512]{2,1,0:T(4,128)(2,1)} %get-tuple-element.9) | copy-start | bytes 24580
  82.5 2.4 %copy-start = (bf16[16,16,2048]{2,1,0:T(8,128)(2,1)S(1)}, bf16[16,16,2048]{2,1,0:T(8,128)(2,1)}, u32[]{:S(2)}) copy-start(bf16[16,16,2048]{2,1,0:T(8,128)(2,1)} %get-tuple-element.11) | copy-start | bytes 3145732

commit v2 on v1

--- a/solution.py
+++ b/solution.py
@@ -37,6 +37,9 @@
 
 T_AR, T_AL, T_HEAD, T_BR, T_BL, T_ROW = 0, 4, 8, 16, 18, 20
 T_OWNPG, T_RECVPG, T_ISOWN, T_INV, T_GROUP, T_LEN, T_PAR = 24, 40, 56, 60, 76, 84, 88
+T_RR, T_RL, T_REC = 96, 98, 100
+PIECES = 4
+REC, REC_X, REC_GATE, REC_MAPS, REC_RAW = 16, 0, 2, 4, 12
 
 
 def dot_nt(a, b, precision=None):
@@ -57,6 +60,17 @@
     return picks
 
 
+def choose_slots(source, base, count, block, most):
+    picks = [jnp.int32(0)] * most
+    seen = jnp.int32(0)
+    for i in range(count):
+        hit = source[base + i] // count == block
+        for k in range(most):
+            picks[k] = jnp.where(hit & (seen == k), i, picks[k])
+        seen = seen + hit.astype(I32)
+    return picks
+
+
 def kernel(ntp, nreq, *refs):
     (
         state_hbm, gain_hbm, pool_hbm, x_hbm, gate_hbm, maps_hbm, q_hbm, entry_hbm,
@@ -65,10 +79,11 @@
         own, a_send, a_recv, rowbuf, b_send, b_recv, pool_v, c_send, c_recv, newp, fin_pool, fin_state,
         gain_in, x_in, gate_in, maps_in, q_in, entry_in,
         p_own, p_recv, p_gain, p_scal, slot_scal, dt_v, decay_v, raw_t,
-        xf, xpad, x_t, qf, ef, maps_f, maps_g, c_rows, outer, member, skip_row, gain_row, stash, ybuf,
-        vis, x_send, x_recv, l_send, l_recv, s_send, s_recv, mixer_v, attn_v, raw_in,
+        xf, rec, r_send, r_recv, recf, xpad, x_t, qf, ef, maps_g, c_rows, outer, member, skip_row, gain_row,
+        stash, ybuf, vis, x_send, l_send, x_pair, l_pair, xc_send, xc_recv, lc_send, lc_recv, lses_v, s_send, s_recv, m_send, m_recv, m_all,
+        mixer_v, attn_v, raw_in,
         rate_s, bias_s, skip_s, old_s, new_s, rsrc, hsrc, ctx, tab,
-        in_sem, scalar_sem, a_ss, a_rs, p_ss, p_rs, b_ss, b_rs, c_ss, c_rs, x_ss, x_rs, l_ss, l_rs, s_ss, s_rs, out_sem,
+        in_sem, scalar_sem, r_ss, r_rs, m_ss, m_rs, a_ss, a_rs, p_ss, p_rs, b_ss, b_rs, c_ss, c_rs, pair_ss, pair_rs, x_ss, x_rs, l_ss, l_rs, s_ss, s_rs, out_sem,
     ) = refs
     share = QH // ntp
     xrows = share * SI
@@ -77,6 +92,31 @@
     t_right, t_left = lax.rem(t + 1, ntp), lax.rem(t + ntp - 1, ntp)
     r_right, r_left = lax.rem(r + 1, nreq), lax.rem(r + nreq - 1, nreq)
     dev = {"tr": (r, t_right), "tl": (r, t_left), "rr": (r_right, t), "rl": (r_left, t)}
+
+    barrier = pltpu.get_barrier_semaphore()
+    for name in ("rr", "rl"):
+        pl.semaphore_signal(barrier, inc=1, device_id=dev[name], device_id_type=MESH)
+
+    def peer(k):
+        core, y_hi = (t + k) % 2, (t // 2 + k // 2) % 2
+        return (t // 4 + k // 4) % (ntp // 4) * 4 + y_hi * 2 + core
+
+    def each_peer(act):
+        def far(n, _):
+            act(n // 2 * 4 + 2 + n % 2)
+            return 0
+
+        def near(n, _):
+            act(n // 2 * 4 + n % 2)
+            return 0
+
+        lax.fori_loop(0, ntp // 2, far, 0)
+        lax.fori_loop(1, ntp // 2, near, 0)
+
+    def greet(k):
+        pl.semaphore_signal(barrier, inc=1, device_id=(r, peer(k)), device_id_type=MESH)
+
+    each_peer(greet)
 
     scalars = [
         pltpu.make_async_copy(src, dst, scalar_sem.at[k])
@@ -101,18 +141,6 @@
     for c in scalars + loads:
         c.start()
 
-    barrier = pltpu.get_barrier_semaphore()
-    for name in ("rr", "rl"):
-        pl.semaphore_signal(barrier, inc=1, device_id=dev[name], device_id_type=MESH)
-
-    def greet(k, _):
-        pl.semaphore_signal(
-            barrier, inc=1, device_id=(r, lax.rem(t + k, ntp)), device_id_type=MESH
-        )
-        return 0
-
-    lax.fori_loop(1, ntp, greet, 0)
-
     with jax.named_scope("scalars"):
         for c in scalars:
             c.wait()
@@ -120,10 +148,66 @@
         tab[T_AR + k] = v
     for k, v in enumerate(choose(hsrc, t_left * HPD, HPD, t, HMV)):
         tab[T_AL + k] = v
+
+    loads[0].wait()
+
+    def pack_a(n, _):
+        d, k, q = n // (HMV * ROWS), (n // ROWS) % HMV, n % ROWS
+        a_send[d, k, q] = own[q, tab[T_AR + d * HMV + k]].astype(BF16)
+        return 0
+
+    lax.fori_loop(0, 2 * HMV * ROWS, pack_a, 0)
+
+    loads[2].wait()
+    sub = lax.broadcasted_iota(I32, (HPD, N), 0)
+    lane = lax.broadcasted_iota(I32, (HPD, N), 1)
+    p_own[0:HPD, 0:P_SIZE] = gain_in[...]
+    wide = p_own[0:HPD, :]
+    p_own[0:HPD, :] = jnp.where(lane < P_SIZE, wide, pltpu.roll(wide, P_SIZE, 1))
+    scal = jnp.zeros((HPD, N), F32)
+    for h in range(HPD):
+        for place, ref in enumerate((bias_s, rate_s, skip_s)):
+            scal = jnp.where((sub == h) & (lane == place), ref[h], scal)
+    p_own[HPD : 2 * HPD, :] = scal
+
+    with jax.named_scope("entry_barrier"):
+        pl.semaphore_wait(barrier, ntp + 1)
+
+    def send(src, dst, ss, rs, to):
+        return pltpu.make_async_remote_copy(
+            src_ref=src, dst_ref=dst, send_sem=ss, recv_sem=rs, device_id=to, device_id_type=MESH
+        )
+
+    a_cp = [
+        send(a_send.at[d], a_recv.at[d], a_ss.at[d], a_rs.at[d], dev[("tr", "tl")[d]])
+        for d in range(2)
+    ]
+    p_cp = [
+        send(p_own, p_recv.at[d], p_ss.at[d], p_rs.at[d], dev[("tr", "tl")[d]]) for d in range(2)
+    ]
+    for c in p_cp + a_cp:
+        c.start()
+
     for k, v in enumerate(choose(rsrc, r_right * ROWS, ROWS, r, MV)):
         tab[T_BR + k] = v
     for k, v in enumerate(choose(rsrc, r_left * ROWS, ROWS, r, MV)):
         tab[T_BL + k] = v
+    for k, v in enumerate(choose_slots(rsrc, r * ROWS, ROWS, r_right, MV)):
+        tab[T_RR + k] = v
+    for k, v in enumerate(choose_slots(rsrc, r * ROWS, ROWS, r_left, MV)):
+        tab[T_RL + k] = v
+    records = [jnp.int32(0)] * ROWS
+    for block, base in ((r_left, ROWS), (r, 0), (r_right, ROWS + MV)):
+        rank = jnp.int32(0)
+        for i in range(ROWS):
+            v = rsrc[block * ROWS + i]
+            hit = v // ROWS == r
+            where = jnp.clip(rank, 0, MV - 1) + base if base else i
+            for q in range(ROWS):
+                records[q] = jnp.where(hit & (v - r * ROWS == q), where, records[q])
+            rank = rank + hit.astype(I32)
+    for q in range(ROWS):
+        tab[T_REC + q] = records[q]
     lefts, rights = jnp.int32(0), jnp.int32(0)
     for j in range(HPD):
         v = hsrc[t * HPD + j]
@@ -150,43 +234,38 @@
         lefts = lefts + (far < 0).astype(I32)
         rights = rights + (far > 0).astype(I32)
 
-    loads[0].wait()
-
-    def pack_a(n, _):
-        d, k, q = n // (HMV * ROWS), (n // ROWS) % HMV, n % ROWS
-        a_send[d, k, q] = own[q, tab[T_AR + d * HMV + k]].astype(BF16)
-        return 0
-
-    lax.fori_loop(0, 2 * HMV * ROWS, pack_a, 0)
-
-    loads[2].wait()
-    sub = lax.broadcasted_iota(I32, (HPD, N), 0)
-    lane = lax.broadcasted_iota(I32, (HPD, N), 1)
-    p_own[0:HPD, 0:P_SIZE] = gain_in[...]
-    wide = p_own[0:HPD, :]
-    p_own[0:HPD, :] = jnp.where(lane < P_SIZE, wide, pltpu.roll(wide, P_SIZE, 1))
-    scal = jnp.zeros((HPD, N), F32)
-    for h in range(HPD):
-        for place, ref in enumerate((bias_s, rate_s, skip_s)):
-            scal = jnp.where((sub == h) & (lane == place), ref[h], scal)
-    p_own[HPD : 2 * HPD, :] = scal
-
-    with jax.named_scope("entry_barrier"):
-        pl.semaphore_wait(barrier, ntp + 1)
-
-    def send(src, dst, ss, rs, to):
-        return pltpu.make_async_remote_copy(
-            src_ref=src, dst_ref=dst, send_sem=ss, recv_sem=rs, device_id=to, device_id_type=MESH
-        )
-
-    a_cp = [
-        send(a_send.at[d], a_recv.at[d], a_ss.at[d], a_rs.at[d], dev[("tr", "tl")[d]])
+    for c in loads[3:6] + loads[8:9]:
+        c.wait()
+    xpad[...] = jnp.zeros_like(xpad)
+    rec[...] = jnp.zeros_like(rec)
+    for s in range(STEPS):
+        xpad[s * ROWS : (s + 1) * ROWS, 0:HPD] = raw_in[s]
+        xf[0, s * ROWS : (s + 1) * ROWS, :] = x_in[s].astype(F32)
+        xf[1, s * ROWS : (s + 1) * ROWS, :] = gate_in[s].astype(F32)
+    for i in range(ROWS):
+        parts = [xf[0, k : k + 1, :] for k in (i, ROWS + i)]
+        parts += [xf[1, k : k + 1, :] for k in (i, ROWS + i)]
+        for s in range(STEPS):
+            maps = maps_in[s, i].astype(F32)
+            for bc in range(2):
+                parts += [maps[bc : bc + 1, h * CH : (h + 1) * CH] for h in range(2)]
+        raws = jnp.concatenate([xpad[i : i + 1, 0:N], xpad[ROWS + i : ROWS + i + 1, 0:N]], axis=1)
+        rest = jnp.concatenate([raws, jnp.zeros((1, CH - 2 * N), F32)], axis=1)
+        for _ in range(3):
+            top = rest.astype(BF16).astype(F32)
+            parts.append(top)
+            rest = rest - top
+        parts.append(rest)
+        rec[i] = jnp.concatenate(parts, axis=0).astype(BF16)
+    for d in range(2):
+        for k in range(MV):
+            r_send[d, k] = rec[tab[T_RR + d * MV + k]]
+
+    r_cp = [
+        send(r_send.at[d], r_recv.at[d], r_ss.at[d], r_rs.at[d], dev[("rr", "rl")[d]])
         for d in range(2)
     ]
-    p_cp = [
-        send(p_own, p_recv.at[d], p_ss.at[d], p_rs.at[d], dev[("tr", "tl")[d]]) for d in range(2)
-    ]
-    for c in p_cp + a_cp:
+    for c in r_cp:
         c.start()
 
     loads[1].wait()
@@ -196,39 +275,28 @@
         c_send[n] = pool_v[old_s[tab[T_BR + d * MV + k], 0, g]]
         return 0
 
+    lax.fori_loop(0, 2 * MV * PGS, pack_c, 0)
+
     c_cp = []
     for d in range(2):
-        lax.fori_loop(d * MV * PGS, (d + 1) * MV * PGS, pack_c, 0)
         part = pl.ds(d * MV * PGS, MV * PGS)
-        c = send(c_send.at[part], c_recv.at[part], c_ss.at[d], c_rs.at[d], dev[("rr", "rl")[d]])
+        c_cp.append(
+            send(c_send.at[part], c_recv.at[part], c_ss.at[d], c_rs.at[d], dev[("rr", "rl")[d]])
+        )
+    for c in c_cp:
         c.start()
-        c_cp.append(c)
 
     for i in range(SLOTS):
         found = jnp.int32(0)
         for e in range(SLOTS):
             found = jnp.where(new_s[e // PGS, 0, e % PGS] == i, e, found)
         tab[T_INV + i] = found
-    for c in loads[3:]:
+    for c in loads[6:8]:
         c.wait()
-    xpad[...] = jnp.zeros_like(xpad)
     for s in range(STEPS):
         part = slice(s * ROWS, (s + 1) * ROWS)
-        xf[0, part, :] = x_in[s].astype(F32)
-        xf[1, part, :] = gate_in[s].astype(F32)
         qf[part, :] = q_in[s].astype(F32)
         ef[part, :] = entry_in[s].astype(F32)
-        for i in range(ROWS):
-            row = 2 * (s * ROWS + i)
-            maps_f[row : row + 2, :] = maps_in[s, i].astype(F32)
-    for g in range(G):
-        maps_g[g] = maps_f[:, g * N : (g + 1) * N]
-    for s in range(STEPS):
-        xpad[s * ROWS : (s + 1) * ROWS, 0:HPD] = raw_in[s]
-    raw_t[...] = xpad[:, 0:N].T[0:HPD, :]
-    xpad[0:SI, :] = xf[0]
-    for m in range(CH // N):
-        x_t[m * N : (m + 1) * N, :] = xpad[:, m * N : (m + 1) * N].T
 
     rowid = lax.broadcasted_iota(I32, (QH, ROWS * PGS * PAGE), 0)
     colid = lax.broadcasted_iota(I32, (QH, ROWS * PGS * PAGE), 1)
@@ -241,7 +309,7 @@
     vis[...] = jnp.where(seen, 1.0, 0.0)
 
     with jax.named_scope("params_arrive"):
-        for c in p_cp:
+        for c in p_cp + r_cp:
             c.wait_recv()
     for part, buf in enumerate((p_gain, p_scal)):
         rows = slice(part * HPD, (part + 1) * HPD)
@@ -251,6 +319,30 @@
     for j in range(HPD):
         slot_scal[j : j + 1, :] = p_scal[pl.ds(tab[T_PAR + j], 1), :]
     bias, rate, skip = (slot_scal[:, k : k + 1] for k in range(3))
+    for q in range(ROWS):
+        at = tab[T_REC + q]
+        mine = rec[jnp.minimum(at, ROWS - 1)].astype(F32)
+        away = jnp.maximum(at - ROWS, 0)
+        came = r_recv[away // MV, away % MV].astype(F32)
+        recf[q] = jnp.where(at < ROWS, mine, came)
+    for q in range(ROWS):
+        raws = recf[q, REC_RAW : REC_RAW + 1, :]
+        for k in range(1, 3):
+            raws = raws + recf[q, REC_RAW + k : REC_RAW + k + 1, :]
+        for s in range(STEPS):
+            k = s * ROWS + q
+            xf[0, k : k + 1, :] = recf[q, REC_X + s : REC_X + s + 1, :]
+            xf[1, k : k + 1, :] = recf[q, REC_GATE + s : REC_GATE + s + 1, :]
+            xpad[k : k + 1, 0:N] = raws[:, s * N : (s + 1) * N]
+            for bc in range(2):
+                for g in range(G):
+                    row = REC_MAPS + (s * 2 + bc) * 2 + g // (G // 2)
+                    lanes = slice(g % (G // 2) * N, (g % (G // 2) + 1) * N)
+                    maps_g[g, 2 * k + bc : 2 * k + bc + 1, :] = recf[q, row : row + 1, lanes]
+    raw_t[...] = xpad[:, 0:N].T[0:HPD, :]
+    xpad[0:SI, :] = xf[0]
+    for m in range(CH // N):
+        x_t[m * N : (m + 1) * N, :] = xpad[:, m * N : (m + 1) * N].T
     v = raw_t[...] + bias
     dt = jnp.maximum(v, 0.0) + jnp.log1p(jnp.exp(-jnp.abs(v)))
     dt_v[...] = dt
@@ -271,7 +363,7 @@
     def prepare(j, _):
         group = tab[T_GROUP + j]
         member[pl.ds(pl.multiple_of(j * P_SIZE, P_SIZE), P_SIZE), :] = jnp.where(
-            lane64 == group, 1.0, 0.0
+            lane64 % G == group, 1.0, 0.0
         )
         both = maps_g[group]
         dts = dt_v[pl.ds(j, 1), :]
@@ -294,12 +386,42 @@
 
     lax.fori_loop(0, 2 * HMV * ROWS, take_a, 0)
 
-    def take_own(n, _):
-        q, j = n // HPD, n % HPD
-        rowbuf[q, j] = own[q, tab[T_HEAD + j]]
-        return 0
-
-    lax.fori_loop(0, ROWS * HPD, take_own, 0)
+    diagonal = lax.broadcasted_iota(I32, (HPD, CH), 0) == (
+        lax.broadcasted_iota(I32, (HPD, CH), 1) // P_SIZE
+    )
+    for i in range(ROWS):
+
+        def step(j, _):
+            now = own[i, tab[T_HEAD + j]]
+            fade = decay_v[pl.ds(j, 1), :]
+            for s in range(STEPS):
+                k = s * ROWS + i
+                now = fade[:, k : k + 1] * now + outer[k, j]
+                stash[s, pl.ds(pl.multiple_of(j * P_SIZE, P_SIZE), P_SIZE), :] = now
+            rowbuf[i, j] = now
+            return 0
+
+        lax.fori_loop(0, HPD, step, 0)
+        for s in range(STEPS):
+            k = s * ROWS + i
+            now = stash[s]
+            top = now.astype(BF16)
+            low = (now - top.astype(F32)).astype(BF16)
+            c8 = c_rows[k].astype(BF16)
+            y = dot_nt(c8, top) + dot_nt(c8, low)
+            ybuf[k : k + 1, :] = jnp.sum(jnp.where(diagonal, y, 0.0), axis=0, keepdims=True)
+
+    gate = xf[1]
+    gated = (ybuf[...] + skip_row[...] * xf[0]) * (gate / (1.0 + jnp.exp(-gate)))
+    packed = sub == lane // G
+    squares = jnp.dot(gated * gated, member[...], precision=HIGH, preferred_element_type=F32)
+    s_send[...] = jnp.sum(jnp.where(packed, squares, 0.0), axis=0, keepdims=True)
+
+    def s_copy(k):
+        return send(s_send, s_recv.at[k], s_ss.at[k], s_rs.at[k], (r, peer(k)))
+
+    each_peer(lambda k: s_copy(k).start())
+    s_recv[0] = s_send[...]
 
     def pack_b(n, _):
         d, k, j = n // (MV * HPD), (n // HPD) % MV, n % HPD
@@ -312,11 +434,13 @@
         for d in range(2)
     ]
 
+    for c in b_cp:
+        c.start()
+
     with jax.named_scope("pages_arrive"):
         for c in c_cp:
             c.wait_recv()
-    for c in b_cp:
-        c.start()
+
     offset = lax.broadcasted_iota(I32, (PAGE, KVW), 0)
 
     def take_page(n, _):
@@ -354,26 +478,79 @@
         lse = jnp.where(total > 0.0, peak + jnp.log(safe), NEG)
         for e in range(per // share):
             rows = slice(e * xrows, (e + 1) * xrows)
-            x_send[g * (per // share) + e] = part[rows]
-            l_send[g * (per // share) + e] = jnp.sum(
+            dest = g * (per // share) + e
+            x_send[dest % 2, dest // 2] = part[rows]
+            l_send[dest % 2, dest // 2] = jnp.sum(
                 jnp.where(eye, lse[rows], 0.0), axis=0, keepdims=True
             )
 
-    def x_copy(k):
-        to = lax.rem(t + k, ntp)
+    side = t % 2
+    other = (r, t + 1 - 2 * side)
+    pair_cp = [
+        send(x_send.at[1 - side], x_pair, pair_ss.at[0], pair_rs.at[0], other),
+        send(l_send.at[1 - side], l_pair, pair_ss.at[1], pair_rs.at[1], other),
+    ]
+    for c in pair_cp:
+        c.start()
+
+    with jax.named_scope("squares_arrive"):
+        each_peer(lambda k: s_copy(k).wait_recv())
+    squares = jnp.sum(s_recv[...], axis=0)
+    scale = jnp.where(packed, lax.rsqrt(squares * (1.0 / GROUP_CHANNELS) + EPSILON), 0.0)
+    mixed = gated * dot_nt(scale, member[...], HIGH) * gain_row[...]
+    for q in range(ROWS):
+        for s in range(STEPS):
+            for m in range(CH // N):
+                k = s * ROWS + q
+                m_all[q, s * (CH // N) + m : s * (CH // N) + m + 1, :] = mixed[
+                    k : k + 1, m * N : (m + 1) * N
+                ]
+    for d in range(2):
+        for k in range(MV):
+            m_send[d, k] = m_all[tab[T_BR + d * MV + k]]
+    m_cp = [
+        send(m_send.at[d], m_recv.at[d], m_ss.at[d], m_rs.at[d], dev[("rr", "rl")[d]])
+        for d in range(2)
+    ]
+    for c in m_cp:
+        c.start()
+
+    with jax.named_scope("pair_arrives"):
+        for c in pair_cp:
+            c.wait_recv()
+    chips = ntp // 2
+    mine, came = l_send[side].reshape(chips, N), l_pair[...].reshape(chips, N)
+    peak = jnp.maximum(mine, came)
+    w_mine, w_came = jnp.exp(mine - peak), jnp.exp(came - peak)
+    total = w_mine + w_came
+    lses_v[...] = peak + jnp.log(total)
+    xpad[0:chips, 0:N] = w_mine / total
+    xpad[chips : 2 * chips, 0:N] = w_came / total
+    cols = xpad[:, 0:N].T
+    for k in range(chips):
+        both = cols[0:xrows, k : k + 1] * x_send[side, k].astype(F32)
+        both = both + cols[0:xrows, chips + k : chips + k + 1] * x_pair[k].astype(F32)
+        xc_send[k] = both.astype(BF16)
+        lc_send[k] = lses_v[k : k + 1, :]
+
+    def x_copies(k):
+        to = peer(2 * k)
         return (
-            send(x_send.at[to], x_recv.at[k], x_ss.at[k], x_rs.at[k], (r, to)),
-            send(l_send.at[to], l_recv.at[k], l_ss.at[k], l_rs.at[k], (r, to)),
+            send(xc_send.at[to // 2], xc_recv.at[k], x_ss.at[k], x_rs.at[k], (r, to)),
+            send(lc_send.at[to // 2], lc_recv.at[k], l_ss.at[k], l_rs.at[k], (r, to)),
         )
 
-    def x_start(k, _):
-        for c in x_copy(k):
-            c.start()
-        return 0
-
-    lax.fori_loop(1, ntp, x_start, 0)
-    x_recv[0] = x_send[t]
-    l_recv[0] = l_send[t]
+    def each_chip(act):
+        def one(k, _):
+            for c in x_copies(k):
+                act(c)
+            return 0
+
+        lax.fori_loop(1, chips, one, 0)
+
+    each_chip(lambda c: c.start())
+    xc_recv[0] = xc_send[t // 2]
+    lc_recv[0] = lc_send[t // 2]
 
     def place_page(n, _):
         fin_pool[n] = newp[tab[T_INV + n]]
@@ -383,20 +560,16 @@
     outs = [pltpu.make_async_copy(fin_pool, pool_out, out_sem.at[0])]
     outs[0].start()
 
-    def x_wait(k, _):
-        for c in x_copy(k):
-            c.wait_recv()
-        return 0
-
     with jax.named_scope("partials_arrive"):
-        lax.fori_loop(1, ntp, x_wait, 0)
-    lses = l_recv[...].reshape(ntp, N)
+        each_chip(lambda c: c.wait_recv())
+    lses = lc_recv[...].reshape(chips, N)
     w = jnp.exp(lses - jnp.max(lses, axis=0, keepdims=True))
     w = w / jnp.sum(w, axis=0, keepdims=True)
+    xpad[0:chips, 0:N] = w
+    cols = xpad[:, 0:N].T
     total = jnp.zeros((xrows, HD), F32)
-    for k in range(ntp):
-        col = jnp.sum(jnp.where(eye, w[k : k + 1, :], 0.0), axis=1, keepdims=True)
-        total = total + col * x_recv[k].astype(F32)
+    for k in range(chips):
+        total = total + cols[0:xrows, k : k + 1] * xc_recv[k].astype(F32)
     for s in range(STEPS):
         for h in range(share):
             attn_v[s, :, h * HD : (h + 1) * HD] = total[
@@ -405,83 +578,69 @@
     outs.append(pltpu.make_async_copy(attn_v, attn_hbm, out_sem.at[1]))
     outs[1].start()
 
+    for c in m_cp:
+        c.wait_recv()
+    for d in range(2):
+        for k in range(MV):
+            m_all[ROWS + d * MV + k] = m_recv[d, k]
+    for i in range(ROWS):
+        row = m_all[tab[T_ROW + i]]
+        for s in range(STEPS):
+            for m in range(CH // N):
+                ybuf[s * ROWS + i : s * ROWS + i + 1, m * N : (m + 1) * N] = row[
+                    s * (CH // N) + m : s * (CH // N) + m + 1
+                ]
+    for s in range(STEPS):
+        mixer_v[s] = ybuf[s * ROWS : (s + 1) * ROWS].astype(BF16)
+    outs.append(pltpu.make_async_copy(mixer_v, mixer_hbm, out_sem.at[2]))
+    outs[2].start()
+
     with jax.named_scope("rows_arrive"):
         for c in b_cp:
             c.wait_recv()
 
-    def take_b(n, _):
-        k, j = n // HPD, n % HPD
-        rowbuf[ROWS + k, j] = b_recv[k // MV, k % MV, j].astype(F32)
+    def place_row(n, _):
+        i, j = n // HPD, n % HPD
+        at = tab[T_ROW + i]
+        away = jnp.maximum(at - ROWS, 0)
+        mine = rowbuf[jnp.minimum(at, ROWS - 1), j]
+        came = b_recv[away // MV, away % MV, j].astype(F32)
+        fin_state[i, j] = jnp.where(at < ROWS, mine, came)
         return 0
 
-    lax.fori_loop(0, 2 * MV * HPD, take_b, 0)
-    diagonal = lax.broadcasted_iota(I32, (HPD, CH), 0) == (
-        lax.broadcasted_iota(I32, (HPD, CH), 1) // P_SIZE
-    )
     for i in range(ROWS):
-
-        def step(j, _):
-            now = rowbuf[tab[T_ROW + i], j]
-            fade = decay_v[pl.ds(j, 1), :]
-            for s in range(STEPS):
-                k = s * ROWS + i
-                now = fade[:, k : k + 1] * now + outer[k, j]
-                stash[s, pl.ds(pl.multiple_of(j * P_SIZE, P_SIZE), P_SIZE), :] = now
-            fin_state[i, j] = now
-            return 0
-
-        lax.fori_loop(0, HPD, step, 0)
-        for s in range(STEPS):
-            k = s * ROWS + i
-            now = stash[s]
-            top = now.astype(BF16)
-            low = (now - top.astype(F32)).astype(BF16)
-            c8 = c_rows[k].astype(BF16)
-            y = dot_nt(c8, top) + dot_nt(c8, low)
-            ybuf[k : k + 1, :] = jnp.sum(jnp.where(diagonal, y, 0.0), axis=0, keepdims=True)
-    outs.append(pltpu.make_async_copy(fin_state, state_out, out_sem.at[2]))
-    outs[2].start()
-
-    gate = xf[1]
-    gated = (ybuf[...] + skip_row[...] * xf[0]) * (gate / (1.0 + jnp.exp(-gate)))
-    s_send[...] = jnp.dot(gated * gated, member[...], precision=HIGH, preferred_element_type=F32)
-
-    def s_copy(k):
-        to = lax.rem(t + k, ntp)
-        return send(s_send, s_recv.at[k], s_ss.at[k], s_rs.at[k], (r, to))
-
-    def s_start(k, _):
-        s_copy(k).start()
-        return 0
-
-    lax.fori_loop(1, ntp, s_start, 0)
-    s_recv[0] = s_send[...]
-
-    def s_wait(k, _):
-        s_copy(k).wait_recv()
-        return 0
-
-    with jax.named_scope("squares_arrive"):
-        lax.fori_loop(1, ntp, s_wait, 0)
-    squares = jnp.sum(s_recv[...], axis=0)
-    scale = lax.rsqrt(squares * (1.0 / GROUP_CHANNELS) + EPSILON)
-    mixed = gated * dot_nt(scale, member[...], HIGH) * gain_row[...]
-    for s in range(STEPS):
-        mixer_v[s] = mixed[s * ROWS : (s + 1) * ROWS].astype(BF16)
-    outs.append(pltpu.make_async_copy(mixer_v, mixer_hbm, out_sem.at[3]))
-    outs[3].start()
-
-    def last(k, _):
-        for c in x_copy(k) + (s_copy(k),):
+        lax.fori_loop(i * HPD, (i + 1) * HPD, place_row, 0)
+        outs.append(pltpu.make_async_copy(fin_state.at[i], state_out.at[i], out_sem.at[3 + i]))
+        outs[3 + i].start()
+
+    with jax.named_scope("all_sent"):
+        for c in a_cp + p_cp + r_cp + c_cp + b_cp + m_cp + pair_cp:
             c.wait_send()
-        return 0
-
-    with jax.named_scope("all_sent"):
-        for c in a_cp + p_cp + c_cp + b_cp:
-            c.wait_send()
-        lax.fori_loop(1, ntp, last, 0)
+        each_peer(lambda k: s_copy(k).wait_send())
+        each_chip(lambda c: c.wait_send())
         for c in outs:
             c.wait()
+
+
+def hand_over(mixer, attn, state, pool, mixer_out, attn_out, state_out, pool_out, m_v, a_v, s_v, p_v, sem):
+    pieces = []
+    for src, mid, dst in ((state, s_v, state_out), (pool, p_v, pool_out)):
+        size = src.shape[0] // PIECES
+        for k in range(PIECES):
+            part = pl.ds(k * size, size)
+            pieces.append((src.at[part], mid.at[part], dst.at[part]))
+    pieces += [(mixer, m_v, mixer_out), (attn, a_v, attn_out)]
+    loads, stores = [], []
+    for k, (src, mid, dst) in enumerate(pieces):
+        loads.append(pltpu.make_async_copy(src, mid, sem.at[0, k]))
+        stores.append(pltpu.make_async_copy(mid, dst, sem.at[1, k]))
+    for c in loads:
+        c.start()
+    for load, store in zip(loads, stores):
+        load.wait()
+        store.start()
+    for c in stores:
+        c.wait()
 
 
 def per_device(ntp, nreq, *arguments):
@@ -497,7 +656,7 @@
         ((ROWS, HPD + 2 * HMV, P_SIZE, N), F32),
         ((2, HMV, ROWS, P_SIZE, N), BF16),
         ((2, HMV, ROWS, P_SIZE, N), BF16),
-        ((ROWS + 2 * MV, HPD, P_SIZE, N), F32),
+        ((ROWS, HPD, P_SIZE, N), F32),
         ((2, MV, HPD, P_SIZE, N), BF16),
         ((2, MV, HPD, P_SIZE, N), BF16),
         ((SLOTS, PAGE, KVW), BF16),
@@ -521,11 +680,14 @@
         ((HPD, N), F32),
         ((HPD, N), F32),
         ((2, SI, CH), F32),
+        ((ROWS, REC, CH), BF16),
+        ((2, MV, REC, CH), BF16),
+        ((2, MV, REC, CH), BF16),
+        ((ROWS, REC, CH), F32),
         ((N, CH), F32),
         ((CH, N), F32),
         ((SI, QH * HD), F32),
         ((SI, KVW), F32),
-        ((2 * SI, G * N), F32),
         ((G, 2 * SI, N), F32),
         ((SI, HPD, N), F32),
         ((SI, HPD, P_SIZE, N), F32),
@@ -535,17 +697,25 @@
         ((STEPS, CH, N), F32),
         ((SI, CH), F32),
         ((QH, SLOTS * PAGE), F32),
-        ((ntp, xrows, HD), BF16),
-        ((ntp, xrows, HD), BF16),
+        ((2, ntp // 2, xrows, HD), BF16),
+        ((2, ntp // 2, 1, N), F32),
+        ((ntp // 2, xrows, HD), BF16),
+        ((ntp // 2, 1, N), F32),
+        ((ntp // 2, xrows, HD), BF16),
+        ((ntp // 2, xrows, HD), BF16),
+        ((ntp // 2, 1, N), F32),
+        ((ntp // 2, 1, N), F32),
+        ((ntp // 2, N), F32),
+        ((1, N), F32),
         ((ntp, 1, N), F32),
-        ((ntp, 1, N), F32),
-        ((SI, N), F32),
-        ((ntp, SI, N), F32),
+        ((2, MV, SI, N), F32),
+        ((2, MV, SI, N), F32),
+        ((ROWS + 2 * MV, SI, N), F32),
         ((STEPS, ROWS, CH), BF16),
         ((STEPS, ROWS, CH), BF16),
         (step_raw.shape, F32),
     ]
-    return pl.pallas_call(
+    results = pl.pallas_call(
         lambda *refs: kernel(ntp, nreq, *refs),
         out_shape=(
             jax.ShapeDtypeStruct((STEPS, ROWS, CH), BF16),
@@ -563,9 +733,9 @@
             pltpu.SMEM((128,), I32),
             dma((9,)),
             dma((8,)),
-            *[dma((2,)) for _ in range(8)],
+            *[dma((2,)) for _ in range(14)],
             *[dma((ntp,)) for _ in range(6)],
-            dma((4,)),
+            dma((3 + ROWS,)),
         ],
         compiler_params=pltpu.CompilerParams(
             collective_id=0, has_side_effects=True, vmem_limit_bytes=63 * 2**20
@@ -576,6 +746,15 @@
         step_raw, decay_rate, step_bias, skip_gain, old_table.transpose(0, 2, 1), new_table.transpose(0, 2, 1),
         request_source, head_source, context_lengths,
     )
+    return pl.pallas_call(
+        hand_over,
+        out_shape=[jax.ShapeDtypeStruct(x.shape, x.dtype) for x in results],
+        in_specs=[anywhere] * 4,
+        out_specs=[anywhere] * 4,
+        scratch_shapes=[pltpu.VMEM(x.shape, x.dtype) for x in results] + [dma((2, 2 + 2 * PIECES))],
+        compiler_params=pltpu.CompilerParams(vmem_limit_bytes=63 * 2**20),
+        name="hand_over",
+    )(*results)
 
 
 def solution(mesh):

time: 86.1 us -> 73.4 us (0.85)
  the two profiles are of different devices: /device:TPU:217 before, /device:TPU:1 now
where the time goes in v2:
time: 73.4 us; the launch traced here: 73.2 us
  Pallas kernels  72.6 us (99%)
    pallas_call x1, Pallas kernels, per_device(): pl.pallas_call(lambda *refs: kernel(ntp, nreq, *refs), out_shape=(jax.Sha...  70.1 us
    pallas_call x1, Pallas kernels, per_device(): pl.pallas_call(hand_over, out_shape=[jax.ShapeDtypeStruct(x.shape, x.dtyp...  2.44 us

profile of v2, /device:TPU:1, one launch (start us, length us, event | category | flops | bytes accessed | tf_op | source)
XLA Modules:
  0.0 73.2 jit_solution(5630925038194829541)
XLA Ops:
  0.6 70.1 %decode.1 = (bf16[2,4,512]{2,1,0:T(4,128)(2,1)}, bf16[2,4,512]{2,1,0:T(4,128)(2,1)}, f32[4,8,64,128]{3,2,1,0:T(8,128)}, bf16[16,16,2048]{2,1,0:T(8,128)(2,1)}) custom-call(f32[4,8,64,128]{3,2,1,0:T(8,128)} %refs_0_.1, f32[8,64]{1,0:T(8,128)} %refs_1_.1, bf16[16,16,2048]{2,1,0:T(8,128)(2,1)} %refs_2_.1, bf16[2,4,512]{2,1,0:T(4,128)(2,1)} %refs_3_.1, ...), custom_call_target="tpu_custom_call" | custom-call | tf_op jit(solution)/shard_map/decode/pallas_call | solution.py:718
  70.8 2.4 %hand_over.1 = (bf16[2,4,512]{2,1,0:T(4,128)(2,1)}, bf16[2,4,512]{2,1,0:T(4,128)(2,1)}, f32[4,8,64,128]{3,2,1,0:T(8,128)}, bf16[16,16,2048]{2,1,0:T(8,128)(2,1)}) custom-call(bf16[2,4,512]{2,1,0:T(4,128)(2,1)} %get-tuple-element.8.mixer, bf16[2,4,512]{2,1,0:T(4,128)(2,1)} %get-tuple-element.9.attn, f32[4,8,64,128]{3,2,1,0:T(8,128)} %get-tuple-element.10.state, ...), custom_call_target="tpu_custom_call" | custom-call | tf_op jit(solution)/shard_map/hand_over/pallas_call | solution.py:749

commit v3 on v2

--- a/solution.py
+++ b/solution.py
@@ -75,15 +75,15 @@
     (
         state_hbm, gain_hbm, pool_hbm, x_hbm, gate_hbm, maps_hbm, q_hbm, entry_hbm,
         raw_hbm, rate_h, bias_h, skip_h, old_h, new_h, rsrc_h, hsrc_h, ctx_h,
-        mixer_hbm, attn_hbm, state_out, pool_out,
-        own, a_send, a_recv, rowbuf, b_send, b_recv, pool_v, c_send, c_recv, newp, fin_pool, fin_state,
+        mixer_v, attn_v, fin_state, fin_pool,
+        own, a_send, a_recv, rowbuf, b_send, b_recv, pool_v, c_send, c_recv, newp,
         gain_in, x_in, gate_in, maps_in, q_in, entry_in,
         p_own, p_recv, p_gain, p_scal, slot_scal, dt_v, decay_v, raw_t,
         xf, rec, r_send, r_recv, recf, xpad, x_t, qf, ef, maps_g, c_rows, outer, member, skip_row, gain_row,
         stash, ybuf, vis, x_send, l_send, x_pair, l_pair, xc_send, xc_recv, lc_send, lc_recv, lses_v, s_send, s_recv, m_send, m_recv, m_all,
-        mixer_v, attn_v, raw_in,
+        raw_in,
         rate_s, bias_s, skip_s, old_s, new_s, rsrc, hsrc, ctx, tab,
-        in_sem, scalar_sem, r_ss, r_rs, m_ss, m_rs, a_ss, a_rs, p_ss, p_rs, b_ss, b_rs, c_ss, c_rs, pair_ss, pair_rs, x_ss, x_rs, l_ss, l_rs, s_ss, s_rs, out_sem,
+        in_sem, scalar_sem, r_ss, r_rs, m_ss, m_rs, a_ss, a_rs, p_ss, p_rs, b_ss, b_rs, c_ss, c_rs, pair_ss, pair_rs, x_ss, x_rs, l_ss, l_rs, s_ss, s_rs,
     ) = refs
     share = QH // ntp
     xrows = share * SI
@@ -92,31 +92,6 @@
     t_right, t_left = lax.rem(t + 1, ntp), lax.rem(t + ntp - 1, ntp)
     r_right, r_left = lax.rem(r + 1, nreq), lax.rem(r + nreq - 1, nreq)
     dev = {"tr": (r, t_right), "tl": (r, t_left), "rr": (r_right, t), "rl": (r_left, t)}
-
-    barrier = pltpu.get_barrier_semaphore()
-    for name in ("rr", "rl"):
-        pl.semaphore_signal(barrier, inc=1, device_id=dev[name], device_id_type=MESH)
-
-    def peer(k):
-        core, y_hi = (t + k) % 2, (t // 2 + k // 2) % 2
-        return (t // 4 + k // 4) % (ntp // 4) * 4 + y_hi * 2 + core
-
-    def each_peer(act):
-        def far(n, _):
-            act(n // 2 * 4 + 2 + n % 2)
-            return 0
-
-        def near(n, _):
-            act(n // 2 * 4 + n % 2)
-            return 0
-
-        lax.fori_loop(0, ntp // 2, far, 0)
-        lax.fori_loop(1, ntp // 2, near, 0)
-
-    def greet(k):
-        pl.semaphore_signal(barrier, inc=1, device_id=(r, peer(k)), device_id_type=MESH)
-
-    each_peer(greet)
 
     scalars = [
         pltpu.make_async_copy(src, dst, scalar_sem.at[k])
@@ -138,12 +113,39 @@
         pltpu.make_async_copy(entry_hbm, entry_in, in_sem.at[7]),
         pltpu.make_async_copy(raw_hbm, raw_in, in_sem.at[8]),
     ]
-    for c in scalars + loads:
+    for c in scalars[:1] + loads[:1]:
+        c.start()
+
+    barrier = pltpu.get_barrier_semaphore()
+    for name in ("rr", "rl"):
+        pl.semaphore_signal(barrier, inc=1, device_id=dev[name], device_id_type=MESH)
+
+    def peer(k):
+        core, y_hi = (t + k) % 2, (t // 2 + k // 2) % 2
+        return (t // 4 + k // 4) % (ntp // 4) * 4 + y_hi * 2 + core
+
+    def each_peer(act):
+        def far(n, _):
+            act(n // 2 * 4 + 2 + n % 2)
+            return 0
+
+        def near(n, _):
+            act(n // 2 * 4 + n % 2)
+            return 0
+
+        lax.fori_loop(0, ntp // 2, far, 0)
+        lax.fori_loop(1, ntp // 2, near, 0)
+
+    def greet(k):
+        pl.semaphore_signal(barrier, inc=1, device_id=(r, peer(k)), device_id_type=MESH)
+
+    each_peer(greet)
+
+    for c in scalars[1:] + loads[1:]:
         c.start()
 
     with jax.named_scope("scalars"):
-        for c in scalars:
-            c.wait()
+        scalars[0].wait()
     for k, v in enumerate(choose(hsrc, t_right * HPD, HPD, t, HMV)):
         tab[T_AR + k] = v
     for k, v in enumerate(choose(hsrc, t_left * HPD, HPD, t, HMV)):
@@ -158,6 +160,23 @@
 
     lax.fori_loop(0, 2 * HMV * ROWS, pack_a, 0)
 
+    with jax.named_scope("entry_barrier"):
+        pl.semaphore_wait(barrier, ntp + 1)
+
+    def send(src, dst, ss, rs, to):
+        return pltpu.make_async_remote_copy(
+            src_ref=src, dst_ref=dst, send_sem=ss, recv_sem=rs, device_id=to, device_id_type=MESH
+        )
+
+    a_cp = [
+        send(a_send.at[d], a_recv.at[d], a_ss.at[d], a_rs.at[d], dev[("tr", "tl")[d]])
+        for d in range(2)
+    ]
+    for c in a_cp:
+        c.start()
+
+    for c in scalars[1:]:
+        c.wait()
     loads[2].wait()
     sub = lax.broadcasted_iota(I32, (HPD, N), 0)
     lane = lax.broadcasted_iota(I32, (HPD, N), 1)
@@ -169,23 +188,10 @@
         for place, ref in enumerate((bias_s, rate_s, skip_s)):
             scal = jnp.where((sub == h) & (lane == place), ref[h], scal)
     p_own[HPD : 2 * HPD, :] = scal
-
-    with jax.named_scope("entry_barrier"):
-        pl.semaphore_wait(barrier, ntp + 1)
-
-    def send(src, dst, ss, rs, to):
-        return pltpu.make_async_remote_copy(
-            src_ref=src, dst_ref=dst, send_sem=ss, recv_sem=rs, device_id=to, device_id_type=MESH
-        )
-
-    a_cp = [
-        send(a_send.at[d], a_recv.at[d], a_ss.at[d], a_rs.at[d], dev[("tr", "tl")[d]])
-        for d in range(2)
-    ]
     p_cp = [
         send(p_own, p_recv.at[d], p_ss.at[d], p_rs.at[d], dev[("tr", "tl")[d]]) for d in range(2)
     ]
-    for c in p_cp + a_cp:
+    for c in p_cp:
         c.start()
 
     for k, v in enumerate(choose(rsrc, r_right * ROWS, ROWS, r, MV)):
@@ -557,8 +563,6 @@
         return 0
 
     lax.fori_loop(0, SLOTS, place_page, 0)
-    outs = [pltpu.make_async_copy(fin_pool, pool_out, out_sem.at[0])]
-    outs[0].start()
 
     with jax.named_scope("partials_arrive"):
         each_chip(lambda c: c.wait_recv())
@@ -575,8 +579,6 @@
             attn_v[s, :, h * HD : (h + 1) * HD] = total[
                 h * SI + s * ROWS : h * SI + (s + 1) * ROWS
             ].astype(BF16)
-    outs.append(pltpu.make_async_copy(attn_v, attn_hbm, out_sem.at[1]))
-    outs[1].start()
 
     for c in m_cp:
         c.wait_recv()
@@ -592,8 +594,6 @@
                 ]
     for s in range(STEPS):
         mixer_v[s] = ybuf[s * ROWS : (s + 1) * ROWS].astype(BF16)
-    outs.append(pltpu.make_async_copy(mixer_v, mixer_hbm, out_sem.at[2]))
-    outs[2].start()
 
     with jax.named_scope("rows_arrive"):
         for c in b_cp:
@@ -608,38 +608,26 @@
         fin_state[i, j] = jnp.where(at < ROWS, mine, came)
         return 0
 
-    for i in range(ROWS):
-        lax.fori_loop(i * HPD, (i + 1) * HPD, place_row, 0)
-        outs.append(pltpu.make_async_copy(fin_state.at[i], state_out.at[i], out_sem.at[3 + i]))
-        outs[3 + i].start()
+    lax.fori_loop(0, ROWS * HPD, place_row, 0)
 
     with jax.named_scope("all_sent"):
         for c in a_cp + p_cp + r_cp + c_cp + b_cp + m_cp + pair_cp:
             c.wait_send()
         each_peer(lambda k: s_copy(k).wait_send())
         each_chip(lambda c: c.wait_send())
-        for c in outs:
-            c.wait()
-
-
-def hand_over(mixer, attn, state, pool, mixer_out, attn_out, state_out, pool_out, m_v, a_v, s_v, p_v, sem):
-    pieces = []
-    for src, mid, dst in ((state, s_v, state_out), (pool, p_v, pool_out)):
+
+
+def hand_over(mixer, attn, state, pool, mixer_out, attn_out, state_out, pool_out, sem):
+    pieces = [(mixer, mixer_out), (attn, attn_out)]
+    for src, dst in ((state, state_out), (pool, pool_out)):
         size = src.shape[0] // PIECES
         for k in range(PIECES):
             part = pl.ds(k * size, size)
-            pieces.append((src.at[part], mid.at[part], dst.at[part]))
-    pieces += [(mixer, m_v, mixer_out), (attn, a_v, attn_out)]
-    loads, stores = [], []
-    for k, (src, mid, dst) in enumerate(pieces):
-        loads.append(pltpu.make_async_copy(src, mid, sem.at[0, k]))
-        stores.append(pltpu.make_async_copy(mid, dst, sem.at[1, k]))
-    for c in loads:
-        c.start()
-    for load, store in zip(loads, stores):
-        load.wait()
-        store.start()
-    for c in stores:
+            pieces.append((src.at[part], dst.at[part]))
+    copies = [pltpu.make_async_copy(a, b, sem.at[k]) for k, (a, b) in enumerate(pieces)]
+    for c in copies:
+        c.start()
+    for c in copies:
         c.wait()
 
 
@@ -663,8 +651,6 @@
         ((2 * MV * PGS, PAGE, KVW), BF16),
         ((2 * MV * PGS, PAGE, KVW), BF16),
         ((SLOTS, PAGE, KVW), BF16),
-        ((SLOTS, PAGE, KVW), BF16),
-        ((ROWS, HPD, P_SIZE, N), F32),
         (norm_gain.shape, F32),
         (mixer_input.shape, BF16),
         (mixer_gate.shape, BF16),
@@ -711,20 +697,18 @@
         ((2, MV, SI, N), F32),
         ((2, MV, SI, N), F32),
         ((ROWS + 2 * MV, SI, N), F32),
-        ((STEPS, ROWS, CH), BF16),
-        ((STEPS, ROWS, CH), BF16),
         (step_raw.shape, F32),
     ]
     results = pl.pallas_call(
         lambda *refs: kernel(ntp, nreq, *refs),
         out_shape=(
-            jax.ShapeDtypeStruct((STEPS, ROWS, CH), BF16),
-            jax.ShapeDtypeStruct((STEPS, ROWS, CH), BF16),
-            jax.ShapeDtypeStruct(scan_state.shape, F32),
-            jax.ShapeDtypeStruct(page_pool.shape, BF16),
+            pltpu.VMEM((STEPS, ROWS, CH), BF16),
+            pltpu.VMEM((STEPS, ROWS, CH), BF16),
+            pltpu.VMEM(scan_state.shape, F32),
+            pltpu.VMEM(page_pool.shape, BF16),
         ),
         in_specs=[pl.BlockSpec(memory_space=pltpu.HBM)] * 17,
-        out_specs=(anywhere,) * 4,
+        out_specs=(pl.BlockSpec(memory_space=pltpu.VMEM),) * 4,
         scratch_shapes=[pltpu.VMEM(shape, dtype) for shape, dtype in scratch]
         + [
             *[pltpu.SMEM((HPD,), F32) for _ in range(3)],
@@ -735,10 +719,9 @@
             dma((8,)),
             *[dma((2,)) for _ in range(14)],
             *[dma((ntp,)) for _ in range(6)],
-            dma((3 + ROWS,)),
         ],
         compiler_params=pltpu.CompilerParams(
-            collective_id=0, has_side_effects=True, vmem_limit_bytes=63 * 2**20
+            collective_id=0, has_side_effects=True, vmem_limit_bytes=60 * 2**20
         ),
         name="decode",
     )(
@@ -751,8 +734,8 @@
         out_shape=[jax.ShapeDtypeStruct(x.shape, x.dtype) for x in results],
         in_specs=[anywhere] * 4,
         out_specs=[anywhere] * 4,
-        scratch_shapes=[pltpu.VMEM(x.shape, x.dtype) for x in results] + [dma((2, 2 + 2 * PIECES))],
-        compiler_params=pltpu.CompilerParams(vmem_limit_bytes=63 * 2**20),
+        scratch_shapes=[dma((2 + 2 * PIECES,))],
+        compiler_params=pltpu.CompilerParams(vmem_limit_bytes=4 * 2**20),
         name="hand_over",
     )(*results)
 

time: 73.4 us -> 71.8 us (0.978)
  Pallas kernels: 72.6 us -> 71 us
    pallas_call x1, Pallas kernels: 2.44 us -> 1.4 us  [per_device(): pl.pallas_call(hand_over, out_shape=[jax.ShapeDtypeStruct(x.shape, x.dtyp...]
where the time goes in v3:
time: 71.8 us; the launch traced here: 71.7 us
  Pallas kernels  71 us (99%)
    pallas_call x1, Pallas kernels, per_device(): pl.pallas_call(lambda *refs: kernel(ntp, nreq, *refs), out_shape=(pltpu.V...  69.6 us

profile of v3, /device:TPU:1, one launch (start us, length us, event | category | flops | bytes accessed | tf_op | source)
XLA Modules:
  0.0 71.7 jit_solution(15270491304449572065)
XLA Ops:
  0.6 69.6 %decode.1 = (bf16[2,4,512]{2,1,0:T(4,128)(2,1)S(1)}, bf16[2,4,512]{2,1,0:T(4,128)(2,1)S(1)}, f32[4,8,64,128]{3,2,1,0:T(8,128)S(1)}, bf16[16,16,2048]{2,1,0:T(8,128)(2,1)S(1)}) custom-call(f32[4,8,64,128]{3,2,1,0:T(8,128)} %refs_0_.1, f32[8,64]{1,0:T(8,128)} %refs_1_.1, bf16[16,16,2048]{2,1,0:T(8,128)(2,1)} %refs_2_.1, bf16[2,4,512]{2,1,0:T(4,128)(2,1)} %refs_3_.1, ...), custom_call_target="tpu_custom_call" | custom-call | tf_op jit(solution)/shard_map/decode/pallas_call | solution.py:702
  70.3 1.4 %hand_over.1 = (bf16[2,4,512]{2,1,0:T(4,128)(2,1)}, bf16[2,4,512]{2,1,0:T(4,128)(2,1)}, f32[4,8,64,128]{3,2,1,0:T(8,128)}, bf16[16,16,2048]{2,1,0:T(8,128)(2,1)}) custom-call(bf16[2,4,512]{2,1,0:T(4,128)(2,1)S(1)} %get-tuple-element.8.mixer, bf16[2,4,512]{2,1,0:T(4,128)(2,1)S(1)} %get-tuple-element.9.attn, f32[4,8,64,128]{3,2,1,0:T(8,128)S(1)} %get-tuple-element.10.state, ...), custom_call_target="tpu_custom_call" | custom-call | tf_op jit(solution)/shard_map/hand_over/pallas_call | solution.py:732

commit v4 on v3

--- a/solution.py
+++ b/solution.py
@@ -167,6 +167,17 @@
         return pltpu.make_async_remote_copy(
             src_ref=src, dst_ref=dst, send_sem=ss, recv_sem=rs, device_id=to, device_id_type=MESH
         )
+
+    run = 4
+    long_way = (lax.rem(r, run) == run - 1, lax.rem(r, run) == 0)
+
+    def start_long(copies):
+        for c, far in zip(copies, long_way):
+            pl.when(far)(c.start)
+
+    def start_short(copies):
+        for c, far in zip(copies, long_way):
+            pl.when(jnp.logical_not(far))(c.start)
 
     a_cp = [
         send(a_send.at[d], a_recv.at[d], a_ss.at[d], a_rs.at[d], dev[("tr", "tl")[d]])
@@ -289,8 +300,7 @@
         c_cp.append(
             send(c_send.at[part], c_recv.at[part], c_ss.at[d], c_rs.at[d], dev[("rr", "rl")[d]])
         )
-    for c in c_cp:
-        c.start()
+    start_long(c_cp)
 
     for i in range(SLOTS):
         found = jnp.int32(0)
@@ -317,6 +327,7 @@
     with jax.named_scope("params_arrive"):
         for c in p_cp + r_cp:
             c.wait_recv()
+    start_short(c_cp)
     for part, buf in enumerate((p_gain, p_scal)):
         rows = slice(part * HPD, (part + 1) * HPD)
         buf[0:HPD, :] = p_recv[0, rows, :]
@@ -440,8 +451,7 @@
         for d in range(2)
     ]
 
-    for c in b_cp:
-        c.start()
+    start_long(b_cp)
 
     with jax.named_scope("pages_arrive"):
         for c in c_cp:
@@ -521,6 +531,7 @@
     for c in m_cp:
         c.start()
 
+    start_short(b_cp)
     with jax.named_scope("pair_arrives"):
         for c in pair_cp:
             c.wait_recv()

time: 71.8 us -> 68.4 us (0.953)
  Pallas kernels: 71 us -> 67.3 us
    pallas_call x1, Pallas kernels: 69.6 us -> 65.9 us  [per_device(): pl.pallas_call(lambda *refs: kernel(ntp, nreq, *refs), out_shape=(pltpu.V...]
where the time goes in v4:
time: 68.4 us; the launch traced here: 67.9 us
  Pallas kernels  67.3 us (98%)
    pallas_call x1, Pallas kernels, per_device(): pl.pallas_call(lambda *refs: kernel(ntp, nreq, *refs), out_shape=(pltpu.V...  65.9 us
    pallas_call x1, Pallas kernels, per_device(): pl.pallas_call(hand_over, out_shape=[jax.ShapeDtypeStruct(x.shape, x.dtyp...  1.4 us

profile of v4, /device:TPU:1, one launch (start us, length us, event | category | flops | bytes accessed | tf_op | source)
XLA Modules:
  0.0 67.9 jit_solution(11444378416233997397)
XLA Ops:
  0.6 65.9 %decode.1 = (bf16[2,4,512]{2,1,0:T(4,128)(2,1)S(1)}, bf16[2,4,512]{2,1,0:T(4,128)(2,1)S(1)}, f32[4,8,64,128]{3,2,1,0:T(8,128)S(1)}, bf16[16,16,2048]{2,1,0:T(8,128)(2,1)S(1)}) custom-call(f32[4,8,64,128]{3,2,1,0:T(8,128)} %refs_0_.1, f32[8,64]{1,0:T(8,128)} %refs_1_.1, bf16[16,16,2048]{2,1,0:T(8,128)(2,1)} %refs_2_.1, bf16[2,4,512]{2,1,0:T(4,128)(2,1)} %refs_3_.1, ...), custom_call_target="tpu_custom_call" | custom-call | tf_op jit(solution)/shard_map/decode/pallas_call | solution.py:713
  66.5 1.4 %hand_over.1 = (bf16[2,4,512]{2,1,0:T(4,128)(2,1)}, bf16[2,4,512]{2,1,0:T(4,128)(2,1)}, f32[4,8,64,128]{3,2,1,0:T(8,128)}, bf16[16,16,2048]{2,1,0:T(8,128)(2,1)}) custom-call(bf16[2,4,512]{2,1,0:T(4,128)(2,1)S(1)} %get-tuple-element.8.mixer, bf16[2,4,512]{2,1,0:T(4,128)(2,1)S(1)} %get-tuple-element.9.attn, f32[4,8,64,128]{3,2,1,0:T(8,128)S(1)} %get-tuple-element.10.state, ...), custom_call_target="tpu_custom_call" | custom-call | tf_op jit(solution)/shard_map/hand_over/pallas_call | solution.py:743
